TPU v7x, 32 devices: a whole 2x2x4 slice. The times are simulated.
32 devices in a mesh: row: 8 (over y, x, core), col: 4 (over z).
Axes of the slice: x: 2, y: 2, z: 4, core: 2. Of those that a mesh axis runs over, the one named last changes fastest.
Arguments:
- object_slices: float32 [2, 2, 1024, 512], P(None, None, 'row', 'col'), may hold values from -4 to 4
- probe_wave: bfloat16 [2, 256, 256], replicated, may hold values from -4 to 4
- propagator_phase: bfloat16 [256, 256], replicated, may hold values from -3.140625 to 3.140625
- intensity: bfloat16 [8, 4, 2, 256, 256], P('row', 'col'), may hold values from 0.099609375 to 3
- centres: int32 [8, 4, 2, 2], P('row', 'col'), may hold values from 0 to 1023, as said below
- batch_order: int32 [8, 4, 2], P('row', 'col'), may hold values from -1 to 30, as said below
Outputs:
- object_gradient: float32 [2, 2, 1024, 512], P(None, None, 'row', 'col')
- probe_gradient: float32 [2, 256, 256], P(None, 'row', 'col')
Inputs may be any that keep to these rules, and one draw needn't show every extreme that they name: `centres`: slot c of tile (g, h) holds (row, column) pixel coordinates in the whole object that lie in that tile: rows g * 128 to (g + 1) * 128 - 1, columns h * 128 to (h + 1) * 128 - 1; empty slots hold a point of their tile too. `batch_order`: -1 marks an empty slot; the live slots of a tile come first and are numbered 0, 1, 2, ... in batch order, tile after tile in row-major order of tiles; some tile has all 2 slots live and some tile has none.
All inputs are finite; a program needn't handle non-finite values.
Results may differ from a plain program's by a relative error of at most 0.0003.
Values sent between devices are 32-bit elements; how exact they have to be, the bound alone decides.
A program may use at most 64 MiB of HBM per device.

v0:
```python
import math

import jax
import jax.numpy as jnp
from jax import lax
from jax.sharding import PartitionSpec as P

PRECISE = lax.Precision.HIGHEST


def with_halo(value, sides, width):
    for axis, dim in sides:
        devices, length = (lax.axis_size(axis), value.shape[dim])
        up = [(i, (i + 1) % devices) for i in range(devices - 1)]
        down = [(j, i) for i, j in up]
        last = lax.slice_in_dim(value, length - width, length, axis=dim)
        leading = lax.slice_in_dim(value, 0, width, axis=dim)
        before = lax.ppermute(last, axis, up)
        after = lax.ppermute(leading, axis, down)
        value = jnp.concatenate([before, value, after], axis=dim)
    return value


def product(left, right):
    return (left[0] * right[0] - left[1] * right[1], left[0] * right[1] + left[1] * right[0])


def conjugate(values):
    return (values[0], -values[1])


def block_table(width, orient):
    first_index = jnp.arange(width, dtype=jnp.int32)[:, None]
    second_index = jnp.arange(width, dtype=jnp.int32)[None, :]
    angles = (first_index * second_index % width).astype(jnp.float32) * (2.0 * math.pi / width)
    factor = 1.0 / math.sqrt(width)
    cosine = jnp.cos(angles) * factor
    sine = orient * jnp.sin(angles) * factor
    real_out = jnp.stack([cosine, -sine])
    imag_out = jnp.stack([sine, cosine])
    return jnp.stack([real_out, imag_out], axis=2)


def transform(values, orient):
    width = values[0].shape[1]
    table = block_table(width, orient)
    stacked = jnp.stack([values[0], values[1]], axis=1)
    once = jnp.einsum("bcaw,cadk->bdkw", stacked, table, precision=PRECISE)
    twice = jnp.einsum("bckw,cwdj->bdkj", once, table, precision=PRECISE)
    return (twice[:, 0], twice[:, 1])


def fold_joint(gradient, half_win):
    received = with_halo(gradient, (("row", 2), ("col", 3)), half_win)
    middle = gradient[:, :, half_win:-half_win, half_win:-half_win]
    inner_rows, inner_cols = (middle.shape[2], middle.shape[3])
    border = 2 * half_win
    middle = middle.at[:, :, :half_win, :].add(
        received[:, :, :half_win, border : border + inner_cols]
    )
    middle = middle.at[:, :, -half_win:, :].add(
        received[:, :, -half_win:, border : border + inner_cols]
    )
    middle = middle.at[:, :, :, :half_win].add(
        received[:, :, border : border + inner_rows, :half_win]
    )
    middle = middle.at[:, :, :, -half_win:].add(
        received[:, :, border : border + inner_rows, -half_win:]
    )
    middle = middle.at[:, :, :half_win, :half_win].add(received[:, :, :half_win, :half_win])
    middle = middle.at[:, :, :half_win, -half_win:].add(received[:, :, :half_win, -half_win:])
    middle = middle.at[:, :, -half_win:, :half_win].add(received[:, :, -half_win:, :half_win])
    middle = middle.at[:, :, -half_win:, -half_win:].add(received[:, :, -half_win:, -half_win:])
    return middle


def per_device(object_slices, probe_wave, propagator_phase, intensity, centres, batch_order):
    slices = object_slices.shape[0]
    tile_rows = object_slices.shape[2]
    tile_cols = object_slices.shape[3]
    width = probe_wave.shape[1]
    half_win = width // 2
    slot_count = centres.shape[2]
    extended = with_halo(object_slices, (("row", 2), ("col", 3)), half_win)
    start_rows = centres[0, 0, :, 0] - lax.axis_index("row") * tile_rows
    start_cols = centres[0, 0, :, 1] - lax.axis_index("col") * tile_cols
    weights = (batch_order[0, 0] >= 0).astype(jnp.float32)[:, None, None]
    zero_index = jnp.zeros((), jnp.int32)

    def cut_window(row_start, col_start):
        return lax.dynamic_slice(
            extended, (zero_index, zero_index, row_start, col_start), (slices, 2, width, width)
        )

    windows = jax.vmap(cut_window)(start_rows, start_cols)
    field_shape = (slot_count, width, width)
    wave_field = (
        jnp.broadcast_to(probe_wave[0].astype(jnp.float32), field_shape),
        jnp.broadcast_to(probe_wave[1].astype(jnp.float32), field_shape),
    )
    angles = propagator_phase.astype(jnp.float32)
    propagator = (jnp.cos(angles)[None], jnp.sin(angles)[None])
    entering = []
    for slice_index in range(slices):
        entering.append(wave_field)
        layer = (windows[:, slice_index, 0], windows[:, slice_index, 1])
        spectrum = transform(product(wave_field, layer), -1.0)
        if slice_index + 1 < slices:
            wave_field = transform(product(spectrum, propagator), 1.0)
    measured = intensity[0, 0].astype(jnp.float32)
    misfit = weights * (spectrum[0] * spectrum[0] + spectrum[1] * spectrum[1] - measured)
    adjoint = transform((misfit * spectrum[0], misfit * spectrum[1]), 1.0)
    object_terms = [None] * slices
    for slice_index in reversed(range(slices)):
        layer = (windows[:, slice_index, 0], windows[:, slice_index, 1])
        object_terms[slice_index] = product(conjugate(entering[slice_index]), adjoint)
        upstream = product(conjugate(layer), adjoint)
        if slice_index > 0:
            adjoint = transform(product(transform(upstream, -1.0), conjugate(propagator)), 1.0)
    stacked = jnp.stack([jnp.stack(term_pair, axis=1) for term_pair in object_terms], axis=1)
    accumulated = jnp.zeros(extended.shape, jnp.float32)
    for slot_index in range(slot_count):
        anchor = (zero_index, zero_index, start_rows[slot_index], start_cols[slot_index])
        current = lax.dynamic_slice(accumulated, anchor, stacked.shape[1:])
        accumulated = lax.dynamic_update_slice(accumulated, current + stacked[slot_index], anchor)
    object_gradient = fold_joint(accumulated, half_win)
    row_count = lax.axis_size("row")
    col_count = lax.axis_size("col")
    block_rows = width // row_count
    block_cols = width // col_count
    probe_term = jnp.stack([jnp.sum(upstream[0], axis=0), jnp.sum(upstream[1], axis=0)])
    probe_term = probe_term.reshape(2, row_count, block_rows, col_count, block_cols)
    probe_term = probe_term.transpose(0, 1, 3, 2, 4).reshape(
        2, row_count * col_count, block_rows * block_cols
    )
    probe_share = lax.psum_scatter(probe_term, ("row", "col"), scatter_dimension=1, tiled=True)
    probe_gradient = probe_share.reshape(2, block_rows, block_cols)
    return (object_gradient, probe_gradient)


def solution(mesh):
    placed = (
        P(None, None, "row", "col"),
        P(),
        P(),
        P("row", "col", None, None, None),
        P("row", "col", None, None),
        P("row", "col", None),
    )
    return jax.shard_map(
        per_device,
        mesh=mesh,
        in_specs=placed,
        out_specs=(P(None, None, "row", "col"), P(None, "row", "col")),
        check_vma=False,
    )
```

profile of v0, /device:TPU:0, one launch (start us, length us, event | category | flops | bytes accessed | tf_op | source)
XLA Modules:
  0.0 300.3 jit_solution(188958492225805551)
XLA Ops:
  7.2 2.5 collective-permute-start
  9.7 1.3 collective-permute-start.1
  11.0 1.7 cosine_multiply_fusion
  12.8 1.9 fusion.54
  15.3 1.0 fusion.68
  16.3 1.7 fusion.52
  18.0 1.8 broadcast_multiply_fusion.1
  25.9 0.9 copy.67
  29.7 4.5 %collective-permute-start.2 = (f32[2,2,384,128]{3,2,1,0:T(8,128)S(1)}, f32[2,2,384,128]{3,2,1,0:T(8,128)S(1)}, u32[]{:S(2)}, u32[]{:S(2)}) collective-permute-start(f32[2,2,384,128]{3,2,1,0:T(8,128)S(1)} %constant_dynamic-update-slice_fusion), channel_id=1, source_target_pairs={{0,1},{1,2},{2,3},{4,5},{5,6},{6,7},{8,9},{9,10},{10,11},{12,13},{... | collective-permute-start | bytes 2359304 | tf_op jit(solution)/shard_map/ppermute | solution.py:18
  34.2 1.3 collective-permute-start.3
  35.5 1.4 fusion.27
  37.0 0.7 fusion.53
  37.7 12.9 %collective-permute-done.2 = f32[2,2,384,128]{3,2,1,0:T(8,128)S(1)} collective-permute-done((f32[2,2,384,128]{3,2,1,0:T(8,128)S(1)}, f32[2,2,384,128]{3,2,1,0:T(8,128)S(1)}, u32[]{:S(2)}, u32[]{:S(2)}) %collective-permute-start.2) | collective-permute-done | bytes 786464 | tf_op jit(solution)/shard_map/ppermute | solution.py:18
  50.6 4.8 %collective-permute-done.3 = f32[2,2,384,128]{3,2,1,0:T(8,128)S(1)} collective-permute-done((f32[2,2,384,128]{3,2,1,0:T(8,128)S(1)}, f32[2,2,384,128]{3,2,1,0:T(8,128)S(1)}, u32[]{:S(2)}, u32[]{:S(2)}) %collective-permute-start.3) | collective-permute-done | bytes 786464 | tf_op jit(solution)/shard_map/ppermute | solution.py:19
  55.4 1.6 pad_maximum_fusion
  56.9 9.4 %while.17 = (s32[]{:T(128)}, f32[2,2,384,384]{3,2,1,0:T(8,128)}, s32[2,4]{1,0:T(2,128)S(1)}, f32[2,2,2,256,256]{4,3,0,2,1:T(8,128)}, s32[]{:T(128)}) while((s32[]{:T(128)}, f32[2,2,384,384]{3,2,1,0:T(8,128)}, s32[2,4]{1,0:T(2,128)S(1)}, f32[2,2,2,256,256]{4,3,0,2,1:T(8,128)}, s32[]{:T(128)}) %tuple.109), condition=%wide.while_cond.8, body=%wide.while_body.8.sunk | while | flops 2 | bytes 2098801 | solution.py:91
  57.6 4.0 %bitcast_dynamic-update-slice_fusion.2 = f32[2,2,2,256,256]{4,3,0,2,1:T(8,128)} fusion(f32[2,2,2,256,256]{4,3,0,2,1:T(8,128)} %get-tuple-element.268, s32[]{:T(128)} %get-tuple-element.265, f32[2,2,384,384]{3,2,1,0:T(8,128)} %get-tuple-element.271, s32[]{:T(128)} %bitcast.281, s32[]{:T(128)} %bitcast.282), kind=kLoop, calls=%fused_computation.clone.1 | loop fusion | bytes 2098688 | tf_op jit(solution)/shard_map/vmap()/gather
  62.3 4.1 %bitcast_dynamic-update-slice_fusion.2 = f32[2,2,2,256,256]{4,3,0,2,1:T(8,128)} fusion(f32[2,2,2,256,256]{4,3,0,2,1:T(8,128)} %get-tuple-element.268, s32[]{:T(128)} %get-tuple-element.265, f32[2,2,384,384]{3,2,1,0:T(8,128)} %get-tuple-element.271, s32[]{:T(128)} %bitcast.281, s32[]{:T(128)} %bitcast.282), kind=kLoop, calls=%fused_computation.clone.1 | loop fusion | bytes 2098688 | tf_op jit(solution)/shard_map/vmap()/gather
  66.4 1.3 fusion.38
  67.7 1.8 convolution_bitcast_fusion.11
  69.5 1.9 convolution_bitcast_fusion.10
  71.5 1.9 convolution_bitcast_fusion.9
  73.4 1.9 convolution_bitcast_fusion.8
  75.4 1.8 convolution_bitcast_fusion.7
  77.3 1.9 convolution_bitcast_fusion.6
  79.4 2.1 convolution_bitcast_fusion.5
  81.4 1.9 convolution_bitcast_fusion.4
  83.6 1.8 convolution_bitcast_fusion.3
  85.5 1.9 convolution_bitcast_fusion.2
  87.5 1.9 convolution_bitcast_fusion.1
  89.4 1.9 convolution_bitcast_fusion
  91.5 0.8 copy-done.1
  92.6 1.2 fusion.1
  94.0 13.4 %dynamic_update_slice.6 = f32[2,2,384,384]{3,2,1,0:T(8,128)S(1)} dynamic-update-slice(f32[2,2,384,384]{3,2,1,0:T(8,128)S(1)} %broadcast_in_dim.8, f32[2,2,256,256]{3,2,1,0:T(8,128)} %fusion.1, s32[]{:T(128)} %constant.298.clone.1, s32[]{:T(128)} %constant.298.clone.1, s32[]{:T(128)S(6)} %select_n.91, s32[]{:T(128)S(6)} %select_n.92) | dynamic-update-slice | bytes 2097156 | tf_op jit(solution)/shard_map/dynamic_update_slice | solution.py:125
  107.5 2.4 fusion.3
  109.9 14.3 %dynamic_update_slice.7 = f32[2,2,384,384]{3,2,1,0:T(8,128)S(1)} dynamic-update-slice(f32[2,2,384,384]{3,2,1,0:T(8,128)S(1)} %dynamic_update_slice.6, f32[2,2,256,256]{3,2,1,0:T(8,128)} %fusion.3, s32[]{:T(128)} %constant.298.clone.1, s32[]{:T(128)} %constant.298.clone.1, s32[]{:T(128)S(6)} %select_n.93, s32[]{:T(128)S(6)} %select_n.94) | dynamic-update-slice | bytes 2097156 | tf_op jit(solution)/shard_map/dynamic_update_slice | solution.py:125
  124.3 2.4 collective-permute-start.4
  126.8 1.6 collective-permute-start.5
  128.6 6.6 %collective-permute-done.5 = f32[2,2,128,384]{3,2,1,0:T(8,128)S(1)} collective-permute-done((f32[2,2,128,384]{3,2,1,0:T(8,128)S(1)}, f32[2,2,128,384]{3,2,1,0:T(8,128)S(1)}, u32[]{:S(2)}, u32[]{:S(2)}) %collective-permute-start.5) | collective-permute-done | bytes 786464 | tf_op jit(solution)/shard_map/ppermute | solution.py:19
  135.2 1.8 pad_maximum_fusion.3
  137.0 5.2 %collective-permute-start.6 = (f32[2,2,640,128]{3,2,1,0:T(8,128)}, f32[2,2,640,128]{3,2,1,0:T(8,128)}, u32[]{:S(2)}, u32[]{:S(2)}) collective-permute-start(f32[2,2,640,128]{3,2,1,0:T(8,128)} %get-tuple-element.186), channel_id=1, source_target_pairs={{0,1},{1,2},{2,3},{4,5},{5,6},{6,7},{8,9},{9,10},{10,11},{12,13},{... | collective-permute-start | bytes 3932168 | tf_op jit(solution)/shard_map/ppermute | solution.py:18
  142.2 1.3 collective-permute-start.7
  143.5 0.9 fusion.30
  144.6 1.2 stack.70
  146.2 1.3 reshape.626
  147.6 142.1 %all-reduce.3.cloned.1.call-done = f32[2,32,2048]{2,0,1:T(2,128)} async-done(((f32[2,32,2048]{2,0,1:T(2,128)}), f32[2,32,2048]{2,0,1:T(2,128)}) %all-reduce.3.cloned.1.call-update) | async-done | bytes 524304
  289.7 0.7 constant_dynamic-slice_fusion.1
  291.1 2.3 slice_add_fusion
  (64 shorter events, 6.9 us)
Async XLA Ops:
  7.2 19.6 %copy-start.10 = (bf16[1,1,2,256,256]{4,3,2,1,0:T(8,128)(2,1)S(1)}, bf16[1,1,2,256,256]{4,3,2,1,0:T(8,128)(2,1)}, u32[]{:S(2)}) copy-start(bf16[1,1,2,256,256]{4,3,2,1,0:T(8,128)(2,1)} %param.41) | copy-start | bytes 786436
  7.2 282.5 %all-reduce.3.cloned.1.call-start = ((), (), s32[]{:S(2)}) async-start(), calls=%async_computation | async-start | bytes 1048576
  7.2 22.4 %collective-permute-start = (f32[2,2,128,128]{3,2,1,0:T(8,128)}, f32[2,2,128,128]{3,2,1,0:T(8,128)S(1)}, u32[]{:S(2)}, u32[]{:S(2)}) collective-permute-start(f32[2,2,128,128]{3,2,1,0:T(8,128)} %param.38), channel_id=1, source_target_pairs={{0,4},{4,8},{8,12},{12,16},{16,20},{20,24},{24,28},{1,5},{5,9},{9,... | collective-permute-start | bytes 786440 | tf_op jit(solution)/shard_map/ppermute | solution.py:18
  9.7 19.9 %collective-permute-start.1 = (f32[2,2,128,128]{3,2,1,0:T(8,128)}, f32[2,2,128,128]{3,2,1,0:T(8,128)S(1)}, u32[]{:S(2)}, u32[]{:S(2)}) collective-permute-start(f32[2,2,128,128]{3,2,1,0:T(8,128)} %param.38), channel_id=1, source_target_pairs={{4,0},{8,4},{12,8},{16,12},{20,16},{24,20},{28,24},{5,1},{9,5},{13... | collective-permute-start | bytes 786440 | tf_op jit(solution)/shard_map/ppermute | solution.py:19
  12.8 16.8 %copy-start.11 = (f32[2,2,128,128]{3,2,1,0:T(8,128)S(1)}, f32[2,2,128,128]{3,2,1,0:T(8,128)}, u32[]{:S(2)}) copy-start(f32[2,2,128,128]{3,2,1,0:T(8,128)} %param.38) | copy-start | bytes 786436
  29.7 7.3 %copy-start.9 = (bf16[2,256,256]{2,1,0:T(8,128)(2,1)S(1)}, bf16[2,256,256]{2,1,0:T(8,128)(2,1)}, u32[]{:S(2)}) copy-start(bf16[2,256,256]{2,1,0:T(8,128)(2,1)} %param.39) | copy-start | bytes 786436
  29.7 20.9 %collective-permute-start.2 = (f32[2,2,384,128]{3,2,1,0:T(8,128)S(1)}, f32[2,2,384,128]{3,2,1,0:T(8,128)S(1)}, u32[]{:S(2)}, u32[]{:S(2)}) collective-permute-start(f32[2,2,384,128]{3,2,1,0:T(8,128)S(1)} %constant_dynamic-update-slice_fusion), channel_id=1, source_target_pairs={{0,1},{1,2},{2,3},{4,5},{5,6},{6,7},{8,9},{9,10},{10,11},{12,13},{... | collective-permute-start | bytes 2359304 | tf_op jit(solution)/shard_map/ppermute | solution.py:18
  34.2 21.2 %collective-permute-start.3 = (f32[2,2,384,128]{3,2,1,0:T(8,128)S(1)}, f32[2,2,384,128]{3,2,1,0:T(8,128)S(1)}, u32[]{:S(2)}, u32[]{:S(2)}) collective-permute-start(f32[2,2,384,128]{3,2,1,0:T(8,128)S(1)} %constant_dynamic-update-slice_fusion), channel_id=1, source_target_pairs={{1,0},{2,1},{3,2},{5,4},{6,5},{7,6},{9,8},{10,9},{11,10},{13,12},{... | collective-permute-start | bytes 2359304 | tf_op jit(solution)/shard_map/ppermute | solution.py:19
  69.5 1.9 copy-start.8
  73.4 1.9 copy-start.3
  89.4 2.0 copy-start.7
  91.2 1.0 copy-start.1
  92.6 1.3 copy-start
  124.3 4.3 %collective-permute-start.4 = (f32[2,2,128,384]{3,2,1,0:T(8,128)S(1)}, f32[2,2,128,384]{3,2,1,0:T(8,128)S(1)}, u32[]{:S(2)}, u32[]{:S(2)}) collective-permute-start(f32[2,2,128,384]{3,2,1,0:T(8,128)S(1)} %get-tuple-element.194), channel_id=1, source_target_pairs={{0,4},{4,8},{8,12},{12,16},{16,20},{20,24},{24,28},{1,5},{5,9},{9,... | collective-permute-start | bytes 2359304 | tf_op jit(solution)/shard_map/ppermute | solution.py:18
  126.8 16.7 %copy-start.2 = (f32[2,2,256,256]{3,2,0,1:T(8,128)S(1)}, f32[2,2,256,256]{3,2,0,1:T(8,128)}, u32[]{:S(2)}) copy-start(f32[2,2,256,256]{3,2,0,1:T(8,128)} %copy-done.1) | copy-start | bytes 3145732
  126.8 16.7 %copy-start.4 = (f32[2,2,2,256,256]{4,3,0,2,1:T(8,128)S(1)}, f32[2,2,2,256,256]{4,3,0,2,1:T(8,128)}, u32[]{:S(2)}) copy-start(f32[2,2,2,256,256]{4,3,0,2,1:T(8,128)} %get-tuple-element.169) | copy-start | bytes 6291460
  126.8 8.4 %collective-permute-start.5 = (f32[2,2,128,384]{3,2,1,0:T(8,128)S(1)}, f32[2,2,128,384]{3,2,1,0:T(8,128)S(1)}, u32[]{:S(2)}, u32[]{:S(2)}) collective-permute-start(f32[2,2,128,384]{3,2,1,0:T(8,128)S(1)} %get-tuple-element.195), channel_id=1, source_target_pairs={{4,0},{8,4},{12,8},{16,12},{20,16},{24,20},{28,24},{5,1},{9,5},{13... | collective-permute-start | bytes 2359304 | tf_op jit(solution)/shard_map/ppermute | solution.py:19
  128.6 8.4 %copy-start.5 = (f32[2,2,128,384]{3,2,1,0:T(8,128)}, f32[2,2,128,384]{3,2,1,0:T(8,128)S(1)}, u32[]{:S(2)}) copy-start(f32[2,2,128,384]{3,2,1,0:T(8,128)S(1)} %collective-permute-done.4) | copy-start | bytes 2359300
  135.2 1.8 copy-start.6
  137.0 154.1 %collective-permute-start.6 = (f32[2,2,640,128]{3,2,1,0:T(8,128)}, f32[2,2,640,128]{3,2,1,0:T(8,128)}, u32[]{:S(2)}, u32[]{:S(2)}) collective-permute-start(f32[2,2,640,128]{3,2,1,0:T(8,128)} %get-tuple-element.186), channel_id=1, source_target_pairs={{0,1},{1,2},{2,3},{4,5},{5,6},{6,7},{8,9},{9,10},{10,11},{12,13},{... | collective-permute-start | bytes 3932168 | tf_op jit(solution)/shard_map/ppermute | solution.py:18
  142.2 149.0 %collective-permute-start.7 = (f32[2,2,640,128]{3,2,1,0:T(8,128)}, f32[2,2,640,128]{3,2,1,0:T(8,128)}, u32[]{:S(2)}, u32[]{:S(2)}) collective-permute-start(f32[2,2,640,128]{3,2,1,0:T(8,128)} %get-tuple-element.187), channel_id=1, source_target_pairs={{1,0},{2,1},{3,2},{5,4},{6,5},{7,6},{9,8},{10,9},{11,10},{13,12},{... | collective-permute-start | bytes 3932168 | tf_op jit(solution)/shard_map/ppermute | solution.py:19
Sparse Core Ops, SparseCore 0:
  147.7 141.9 all-reduce.2
where the time goes:
time: 301 us; the launch traced here: 300 us
  waiting for transfers between devices  167 us (55%)
  local copies, waits for them, and re-layouts  44.8 us (15%)
  other arithmetic  24.1 us (8%)
  matrix products  22.5 us (7%)
  between operations  22.3 us (7%)
  starting transfers between devices  20 us (7%)
    unnamed x2, waiting for transfers between devices  142 us
    dynamic_update_slice x2, local copies, waits for them, and re-layouts, per_device(): lax.dynamic_update_slice(accumulated, current + stacked[slot_index], anchor)  27.8 us
    ppermute x4, starting transfers between devices, with_halo(): before = lax.ppermute(last, axis, up)  14.6 us
    ppermute x4, waiting for transfers between devices, with_halo(): before = lax.ppermute(last, axis, up)  13.1 us
    ppermute x4, waiting for transfers between devices, with_halo(): after = lax.ppermute(leading, axis, down)  11.4 us
    dot_general x6, matrix products, transform(): once = jnp.einsum('bcaw,cadk->bdkw', stacked, table, precision=PRECISE)  11.3 us
    dot_general x6, matrix products, transform(): twice = jnp.einsum('bckw,cwdj->bdkj', once, table, precision=PRECISE)  11.2 us
    gather x6, local copies, waits for them, and re-layouts  9.4 us
  transfers between devices with their start and end apart: 9, of which 5 were waited for; matrix products, arithmetic and copies ran while one was open for 6% of the time, Pallas kernels for 0%

commit v1 on v0

v1 whole, which is shorter than its diff:
```python
import functools
import math

import jax
import jax.numpy as jnp
import ml_dtypes
import numpy as np
from jax import lax
from jax.experimental import pallas as pl
from jax.experimental.pallas import tpu as pltpu
from jax.sharding import PartitionSpec as P


def shift_pair(value, axis, dim, width):
    devices, length = (lax.axis_size(axis), value.shape[dim])
    up = [(i, (i + 1) % devices) for i in range(devices - 1)]
    down = [(j, i) for i, j in up]
    last = lax.slice_in_dim(value, length - width, length, axis=dim)
    leading = lax.slice_in_dim(value, 0, width, axis=dim)
    return lax.ppermute(last, axis, up), lax.ppermute(leading, axis, down)


def with_halo(value, sides, width):
    for axis, dim in sides:
        before, after = shift_pair(value, axis, dim, width)
        value = jnp.concatenate([before, value, after], axis=dim)
    return value


def fold(value, sides, width):
    for axis, dim in sides:
        before, after = shift_pair(value, axis, dim, width)
        length = value.shape[dim] - 2 * width
        middle = lax.slice_in_dim(value, width, width + length, axis=dim)
        if length == width:
            value = middle + before + after
        else:
            pads = [(0, 0)] * value.ndim
            pads[dim] = (0, length - width)
            first = jnp.pad(before, pads)
            pads[dim] = (length - width, 0)
            value = middle + first + jnp.pad(after, pads)
    return value


def halve(value, axis, dim):
    devices = lax.axis_size(axis)
    index = lax.axis_index(axis)
    bits = devices.bit_length() - 1
    shape = value.shape
    value = value.reshape(shape[:dim] + (2,) * bits + (shape[dim] // devices,) + shape[dim + 1 :])
    for bit in range(bits):
        at = dim + bits - 1 - bit
        mine = lax.rem(index // (1 << bit), 2)
        kept = lax.dynamic_index_in_dim(value, mine, at, keepdims=False)
        sent = lax.dynamic_index_in_dim(value, 1 - mine, at, keepdims=False)
        pairs = [(i, i ^ (1 << bit)) for i in range(devices)]
        value = kept + lax.ppermute(sent, axis, pairs)
    return value


def split(value):
    high = value.astype(jnp.bfloat16)
    low = (value - high.astype(jnp.float32)).astype(jnp.bfloat16)
    return high, low


def tables(width):
    index = np.arange(width)
    angles = (np.outer(index, index) % width) * (2.0 * math.pi / width)
    cosine = np.cos(angles) / math.sqrt(width)
    sine = np.sin(angles) / math.sqrt(width)
    out = []
    for orient in (-1.0, 1.0):
        block = np.block([[cosine, orient * sine], [-orient * sine, cosine]]).astype(np.float32)
        high = block.astype(ml_dtypes.bfloat16)
        low = (block - high.astype(np.float32)).astype(ml_dtypes.bfloat16)
        out += [high, low]
    return out


def dot(left, right):
    return jnp.dot(left, right, preferred_element_type=jnp.float32)


def make_transform(forward, inverse, width):
    def transform(values, orient):
        first, second = (forward, inverse) if orient < 0 else (inverse, forward)
        high, low = split(jnp.concatenate(values, axis=1))
        table = first[0][...]
        once = dot(high, table) + dot(low, table) + dot(high, first[1][...])
        high, low = split(jnp.concatenate([once[:, :width], once[:, width:]], axis=0))
        table = second[0][...]
        twice = dot(table, high) + dot(table, low) + dot(second[1][...], high)
        return (twice[:width], twice[width:])

    return transform


def product(left, right):
    return (left[0] * right[0] - left[1] * right[1], left[0] * right[1] + left[1] * right[0])


def conjugate(values):
    return (values[0], -values[1])


def kernel(starts, live, ext, probe, prop, intensity, fh, fl, ih, il, grad, pgrad, padded):
    slices = ext.shape[0]
    width = probe.shape[1]
    rows, cols = ext.shape[2], ext.shape[3]
    slot_count = intensity.shape[0]
    transform = make_transform((fh, fl), (ih, il), width)
    grad[...] = jnp.zeros_like(grad)
    pgrad[...] = jnp.zeros_like(pgrad)
    padded[...] = jnp.zeros_like(padded)

    def slot_body(slot, carry):
        row = starts[slot, 0]
        col = starts[slot, 1]

        def window(s):
            parts = []
            for c in range(2):
                band = pltpu.roll(ext[s, c], lax.rem(rows - row, rows), 0)[:width]
                parts.append(pltpu.roll(band, lax.rem(cols - col, cols), 1)[:, :width])
            return tuple(parts)

        def place(s, values):
            for c in range(2):
                padded[:width, :width] = values[c]
                band = pltpu.roll(padded[...], row, 0)
                grad[s, c] += pltpu.roll(band, col, 1)

        field = (probe[0].astype(jnp.float32), probe[1].astype(jnp.float32))
        propagator = (prop[0], prop[1])
        layers, entering = [], []
        for s in range(slices):
            entering.append(field)
            layers.append(window(s))
            spectrum = transform(product(field, layers[s]), -1.0)
            if s + 1 < slices:
                field = transform(product(spectrum, propagator), 1.0)
        measured = intensity[slot].astype(jnp.float32)
        weight = jnp.where(live[slot] >= 0, 1.0, 0.0).astype(jnp.float32)
        misfit = weight * (spectrum[0] * spectrum[0] + spectrum[1] * spectrum[1] - measured)
        adjoint = transform((misfit * spectrum[0], misfit * spectrum[1]), 1.0)
        for s in reversed(range(slices)):
            place(s, product(conjugate(entering[s]), adjoint))
            upstream = product(conjugate(layers[s]), adjoint)
            if s > 0:
                adjoint = transform(
                    product(transform(upstream, -1.0), conjugate(propagator)), 1.0
                )
        pgrad[0] += upstream[0]
        pgrad[1] += upstream[1]
        return carry

    lax.fori_loop(0, slot_count, slot_body, 0)


def gradients(starts, live, extended, probe, prop, intensity):
    width = probe.shape[1]
    rows, cols = extended.shape[2:]
    smem = pl.BlockSpec(memory_space=pltpu.SMEM)
    vmem = pl.BlockSpec(memory_space=pltpu.VMEM)
    flops = intensity.shape[0] * 6 * 2 * 3 * 2 * width * 4 * width * width
    return pl.pallas_call(
        kernel,
        out_shape=(
            jax.ShapeDtypeStruct(extended.shape, jnp.float32),
            jax.ShapeDtypeStruct((2, width, width), jnp.float32),
        ),
        in_specs=[smem] * 2 + [vmem] * 8,
        out_specs=(vmem, vmem),
        scratch_shapes=[pltpu.VMEM((rows, cols), jnp.float32)],
        compiler_params=pltpu.CompilerParams(vmem_limit_bytes=48 * 2**20),
        cost_estimate=pl.CostEstimate(flops=flops, bytes_accessed=10 * 2**20, transcendentals=0),
    )(starts, live, extended, probe, prop, intensity, *tables(width))


def per_device(object_slices, probe_wave, propagator_phase, intensity, centres, batch_order):
    tile_rows, tile_cols = object_slices.shape[2:]
    width = probe_wave.shape[1]
    half_win = width // 2
    extended = with_halo(object_slices, (("row", 2), ("col", 3)), half_win)
    origin = jnp.stack([lax.axis_index("row") * tile_rows, lax.axis_index("col") * tile_cols])
    starts = (centres[0, 0] - origin[None]).astype(jnp.int32)
    angles = propagator_phase.astype(jnp.float32)
    prop = jnp.stack([jnp.cos(angles), jnp.sin(angles)])
    accumulated, probe_term = gradients(
        starts, batch_order[0, 0], extended, probe_wave, prop, intensity[0, 0]
    )
    object_gradient = fold(accumulated, (("col", 3), ("row", 2)), half_win)
    probe_gradient = halve(halve(probe_term, "row", 1), "col", 2)
    return (object_gradient, probe_gradient)


def solution(mesh):
    placed = (
        P(None, None, "row", "col"),
        P(),
        P(),
        P("row", "col", None, None, None),
        P("row", "col", None, None),
        P("row", "col", None),
    )
    return jax.shard_map(
        per_device,
        mesh=mesh,
        in_specs=placed,
        out_specs=(P(None, None, "row", "col"), P(None, "row", "col")),
        check_vma=False,
    )
```

time: 301 us -> 105 us (0.35)
  the two profiles are of different devices: /device:TPU:0 before, /device:TPU:28 now
where the time goes in v1:
time: 105 us
  waiting for transfers between devices  49 us (47%)
  Pallas kernels  24.6 us (23%)
  starting transfers between devices  19.2 us (18%)
  other arithmetic  6.45 us (6%)
  local copies, waits for them, and re-layouts  4.34 us (4%)
    ppermute x8, waiting for transfers between devices, shift_pair(): return (lax.ppermute(last, axis, up), lax.ppermute(leading, axis, down))  30.2 us
    pallas_call x1, Pallas kernels, gradients(): pl.pallas_call(kernel, out_shape=(jax.ShapeDtypeStruct(extended.shape, jn...  24.6 us
    ppermute x5, waiting for transfers between devices, halve(): value = kept + lax.ppermute(sent, axis, pairs)  18.8 us
    ppermute x8, starting transfers between devices, shift_pair(): return (lax.ppermute(last, axis, up), lax.ppermute(leading, axis, down))  18.1 us
    add x2, other arithmetic, fold(): value = middle + before + after  2.23 us
  transfers between devices with their start and end apart: 13, of which 10 were waited for; matrix products, arithmetic and copies ran while one was open for 6% of the time, Pallas kernels for 0%

profile of v1, /device:TPU:28, one launch (start us, length us, event | category | flops | bytes accessed | tf_op | source)
XLA Modules:
  0.0 104.6 jit_solution(12611987654566027458)
XLA Ops:
  0.6 0.0 copy-start.8
  0.6 1.9 %collective-permute-start = (f32[2,2,128,128]{3,2,1,0:T(8,128)}, f32[2,2,128,128]{3,2,1,0:T(8,128)S(1)}, u32[]{:S(2)}, u32[]{:S(2)}) collective-permute-start(f32[2,2,128,128]{3,2,1,0:T(8,128)} %param.10), channel_id=1, source_target_pairs={{0,4},{4,8},{8,12},{12,16},{16,20},{20,24},{24,28},{1,5},{5,9},{9,... | collective-permute-start | bytes 786440 | tf_op jit(solution)/shard_map/ppermute | solution.py:20
  2.6 4.5 %collective-permute-start.1 = (f32[2,2,128,128]{3,2,1,0:T(8,128)}, f32[2,2,128,128]{3,2,1,0:T(8,128)S(1)}, u32[]{:S(2)}, u32[]{:S(2)}) collective-permute-start(f32[2,2,128,128]{3,2,1,0:T(8,128)} %param.10), channel_id=1, source_target_pairs={{4,0},{8,4},{12,8},{16,12},{20,16},{24,20},{28,24},{5,1},{9,5},{13... | collective-permute-start | bytes 786440 | tf_op jit(solution)/shard_map/ppermute | solution.py:20
  7.1 2.3 %collective-permute-done = f32[2,2,128,128]{3,2,1,0:T(8,128)S(1)} collective-permute-done((f32[2,2,128,128]{3,2,1,0:T(8,128)}, f32[2,2,128,128]{3,2,1,0:T(8,128)S(1)}, u32[]{:S(2)}, u32[]{:S(2)}) %collective-permute-start) | collective-permute-done | bytes 262176 | tf_op jit(solution)/shard_map/ppermute | solution.py:20
  9.5 1.0 constant_dynamic-update-slice_fusion.1
  10.4 0.9 collective-permute-done.1
  11.3 2.4 %collective-permute-start.3 = (f32[2,2,384,128]{3,2,1,0:T(8,128)S(1)}, f32[2,2,384,128]{3,2,1,0:T(8,128)S(1)}, u32[]{:S(2)}, u32[]{:S(2)}) collective-permute-start(f32[2,2,384,128]{3,2,1,0:T(8,128)S(1)} %constant_dynamic-update-slice_fusion), channel_id=1, source_target_pairs={{1,0},{2,1},{3,2},{5,4},{6,5},{7,6},{9,8},{10,9},{11,10},{13,12},{... | collective-permute-start | bytes 2359304 | tf_op jit(solution)/shard_map/ppermute | solution.py:20
  13.7 1.3 %collective-permute-start.2 = (f32[2,2,384,128]{3,2,1,0:T(8,128)S(1)}, f32[2,2,384,128]{3,2,1,0:T(8,128)S(1)}, u32[]{:S(2)}, u32[]{:S(2)}) collective-permute-start(f32[2,2,384,128]{3,2,1,0:T(8,128)S(1)} %constant_dynamic-update-slice_fusion), channel_id=1, source_target_pairs={{0,1},{1,2},{2,3},{4,5},{5,6},{6,7},{8,9},{9,10},{10,11},{12,13},{... | collective-permute-start | bytes 2359304 | tf_op jit(solution)/shard_map/ppermute | solution.py:20
  15.1 0.1 pad_add_fusion
  15.2 1.8 %fusion = (f32[1,256,256]{2,1,0:T(8,128)S(1)}, f32[1,256,256]{2,1,0:T(8,128)S(1)}) fusion(bf16[256,256]{1,0:T(8,128)(2,1)} %param.12), kind=kLoop, calls=%fused_computation.5 | loop fusion | flops 65536 | bytes 655360 | tf_op jit(solution)/shard_map/stack | solution.py:190
  17.0 0.0 copy-start
  17.0 0.0 copy-start.1
  17.1 0.0 copy-start.2
  17.1 0.0 copy-start.3
  17.1 0.0 copy-start.4
  17.1 0.0 copy-start.5
  17.1 0.0 copy-start.6
  17.1 14.3 %collective-permute-done.3 = f32[2,2,384,128]{3,2,1,0:T(8,128)S(1)} collective-permute-done((f32[2,2,384,128]{3,2,1,0:T(8,128)S(1)}, f32[2,2,384,128]{3,2,1,0:T(8,128)S(1)}, u32[]{:S(2)}, u32[]{:S(2)}) %collective-permute-start.3) | collective-permute-done | bytes 786464 | tf_op jit(solution)/shard_map/ppermute | solution.py:20
  31.4 4.2 %collective-permute-done.2 = f32[2,2,384,128]{3,2,1,0:T(8,128)S(1)} collective-permute-done((f32[2,2,384,128]{3,2,1,0:T(8,128)S(1)}, f32[2,2,384,128]{3,2,1,0:T(8,128)S(1)}, u32[]{:S(2)}, u32[]{:S(2)}) %collective-permute-start.2) | collective-permute-done | bytes 786464 | tf_op jit(solution)/shard_map/ppermute | solution.py:20
  35.6 1.6 %pad_maximum_fusion.ext = f32[2,2,384,384]{3,2,1,0:T(8,128)} fusion(f32[2,2,384,128]{3,2,1,0:T(8,128)S(1)} %collective-permute-done.3, f32[2,2,384,128]{3,2,1,0:T(8,128)S(1)} %constant_dynamic-update-slice_fusion, f32[2,2,384,128]{3,2,1,0:T(8,128)S(1)} %collective-permute-done.2), kind=kLoop, calls=%fused_computation | loop fusion | flops 1179648 | bytes 4718592 | tf_op jit(solution)/shard_map/concatenate | solution.py:26
  37.2 24.6 %shard_map.113 = (f32[2,2,384,384]{3,2,1,0:T(8,128)S(1)}, f32[2,256,256]{2,1,0:T(8,128)S(1)}) custom-call(s32[2,2]{1,0:T(2,128)S(1)} %bitcast_subtract_fusion.starts, s32[2]{0:T(128)S(1)} %bitcast.31, f32[2,2,384,384]{3,2,1,0:T(8,128)} %pad_maximum_fusion.ext, bf16[2,256,256]{2,1,0:T(8,128)(2,1)S(1)} %copy-done, f32[2,256,256]{2,1,0:T(8,128)S(1)} %pad_maximum_fusion.1.prop, ...), custom_call_target="tpu_custom_call" | custom-call | flops 9663676416 | bytes 10485760 | tf_op jit(solution)/shard_map/pallas_call | solution.py:168
  61.8 0.1 collective-permute-start.8
  61.9 1.3 %fusion.3 = (f32[2,2,384,128]{3,2,1,0:T(8,128)}, f32[2,2,384,128]{3,2,1,0:T(8,128)}) fusion(f32[2,2,384,384]{3,2,1,0:T(8,128)S(1)} %get-tuple-element.4), kind=kLoop, calls=%fused_computation.26 | loop fusion | bytes 3145728 | tf_op jit(solution)/shard_map/slice | solution.py:18
  63.2 2.4 %collective-permute-start.5 = (f32[2,2,384,128]{3,2,1,0:T(8,128)}, f32[2,2,384,128]{3,2,1,0:T(8,128)S(1)}, u32[]{:S(2)}, u32[]{:S(2)}) collective-permute-start(f32[2,2,384,128]{3,2,1,0:T(8,128)} %get-tuple-element.7), channel_id=1, source_target_pairs={{1,0},{2,1},{3,2},{5,4},{6,5},{7,6},{9,8},{10,9},{11,10},{13,12},{... | collective-permute-start | bytes 2359304 | tf_op jit(solution)/shard_map/ppermute | solution.py:20
  65.5 1.3 %collective-permute-start.4 = (f32[2,2,384,128]{3,2,1,0:T(8,128)}, f32[2,2,384,128]{3,2,1,0:T(8,128)}, u32[]{:S(2)}, u32[]{:S(2)}) collective-permute-start(f32[2,2,384,128]{3,2,1,0:T(8,128)} %get-tuple-element.6), channel_id=1, source_target_pairs={{0,1},{1,2},{2,3},{4,5},{5,6},{6,7},{8,9},{9,10},{10,11},{12,13},{... | collective-permute-start | bytes 2359304 | tf_op jit(solution)/shard_map/ppermute | solution.py:20
  66.8 0.0 collective-permute-done.8
  66.9 0.7 copy.16
  67.6 0.0 collective-permute-start.9
  67.6 5.8 %collective-permute-done.9 = f32[2,2,32,256]{3,2,0,1:T(8,128)S(1)} collective-permute-done((f32[2,2,32,256]{3,2,0,1:T(8,128)}, f32[2,2,32,256]{3,2,0,1:T(8,128)S(1)}, u32[]{:S(2)}, u32[]{:S(2)}) %collective-permute-start.9) | collective-permute-done | bytes 131104 | tf_op jit(solution)/shard_map/ppermute | solution.py:58
  73.5 0.1 collective-permute-start.10
  73.5 4.2 %collective-permute-done.10 = f32[2,32,256]{2,1,0:T(8,128)S(1)} collective-permute-done((f32[2,32,256]{2,1,0:T(8,128)S(1)}, f32[2,32,256]{2,1,0:T(8,128)S(1)}, u32[]{:S(2)}, u32[]{:S(2)}) %collective-permute-start.10) | collective-permute-done | bytes 65568 | tf_op jit(solution)/shard_map/ppermute | solution.py:58
  77.8 0.1 reshape.12
  77.9 5.3 %collective-permute-done.5 = f32[2,2,384,128]{3,2,1,0:T(8,128)S(1)} collective-permute-done((f32[2,2,384,128]{3,2,1,0:T(8,128)}, f32[2,2,384,128]{3,2,1,0:T(8,128)S(1)}, u32[]{:S(2)}, u32[]{:S(2)}) %collective-permute-start.5) | collective-permute-done | bytes 786464 | tf_op jit(solution)/shard_map/ppermute | solution.py:20
  83.2 0.9 copy-done.7
  84.1 3.3 %collective-permute-done.4 = f32[2,2,384,128]{3,2,1,0:T(8,128)} collective-permute-done((f32[2,2,384,128]{3,2,1,0:T(8,128)}, f32[2,2,384,128]{3,2,1,0:T(8,128)}, u32[]{:S(2)}, u32[]{:S(2)}) %collective-permute-start.4) | collective-permute-done | bytes 786464 | tf_op jit(solution)/shard_map/ppermute | solution.py:20
  87.4 1.5 %add_add_fusion = f32[2,2,384,128]{3,2,1,0:T(8,128)S(1)} fusion(f32[2,2,384,128]{3,2,1,0:T(8,128)} %copy-done.7, f32[2,2,384,128]{3,2,1,0:T(8,128)} %collective-permute-done.4, f32[2,2,384,384]{3,2,1,0:T(8,128)S(1)} %get-tuple-element.4), kind=kLoop, calls=%fused_computation.1 | loop fusion | flops 393216 | bytes 3145728 | tf_op jit(solution)/shard_map/add | solution.py:36
  88.9 1.9 %collective-permute-start.7 = (f32[2,2,128,128]{3,2,1,0:T(8,128)S(1)}, f32[2,2,128,128]{3,2,1,0:T(8,128)S(1)}, u32[]{:S(2)}, u32[]{:S(2)}) collective-permute-start(f32[2,2,128,128]{3,2,1,0:T(8,128)S(1)} %get-tuple-element.9), channel_id=1, source_target_pairs={{4,0},{8,4},{12,8},{16,12},{20,16},{24,20},{28,24},{5,1},{9,5},{13... | collective-permute-start | bytes 786440 | tf_op jit(solution)/shard_map/ppermute | solution.py:20
  90.9 2.4 %collective-permute-start.6 = (f32[2,2,128,128]{3,2,1,0:T(8,128)S(1)}, f32[2,2,128,128]{3,2,1,0:T(8,128)S(1)}, u32[]{:S(2)}, u32[]{:S(2)}) collective-permute-start(f32[2,2,128,128]{3,2,1,0:T(8,128)S(1)} %get-tuple-element.8), channel_id=1, source_target_pairs={{0,4},{4,8},{8,12},{12,16},{16,20},{20,24},{24,28},{1,5},{5,9},{9,... | collective-permute-start | bytes 786440 | tf_op jit(solution)/shard_map/ppermute | solution.py:20
  93.3 0.1 constant_dynamic-slice_fusion.2
  93.4 0.5 collective-permute-start.11
  93.9 4.2 %collective-permute-done.11 = f32[2,32,2,64]{3,2,1,0:T(2,128)S(1)} collective-permute-done((f32[2,32,2,64]{3,2,1,0:T(2,128)S(1)}, f32[2,32,2,64]{3,2,1,0:T(2,128)S(1)}, u32[]{:S(2)}, u32[]{:S(2)}) %collective-permute-start.11) | collective-permute-done | bytes 32800 | tf_op jit(solution)/shard_map/ppermute | solution.py:58
  98.1 0.1 constant_dynamic-slice_fusion
  98.2 0.5 collective-permute-start.12
  98.7 4.6 %collective-permute-done.12 = f32[2,32,64]{2,1,0:T(8,128)S(1)} collective-permute-done((f32[2,32,64]{2,1,0:T(8,128)S(1)}, f32[2,32,64]{2,1,0:T(8,128)S(1)}, u32[]{:S(2)}, u32[]{:S(2)}) %collective-permute-start.12) | collective-permute-done | bytes 16416 | tf_op jit(solution)/shard_map/ppermute | solution.py:58
  103.3 0.6 add.90
  103.9 0.0 collective-permute-done.7
  103.9 0.0 collective-permute-done.6
  103.9 0.7 fusion.2
  (21 shorter events, 0.3 us)
Async XLA Ops:
  0.6 16.4 %copy-start.8 = (s32[1,1,2,2]{3,2,1,0:T(2,128)S(1)}, s32[1,1,2,2]{3,2,1,0:T(2,128)}, u32[]{:S(2)}) copy-start(s32[1,1,2,2]{3,2,1,0:T(2,128)} %param.14) | copy-start | bytes 52
  0.6 8.8 %collective-permute-start = (f32[2,2,128,128]{3,2,1,0:T(8,128)}, f32[2,2,128,128]{3,2,1,0:T(8,128)S(1)}, u32[]{:S(2)}, u32[]{:S(2)}) collective-permute-start(f32[2,2,128,128]{3,2,1,0:T(8,128)} %param.10), channel_id=1, source_target_pairs={{0,4},{4,8},{8,12},{12,16},{16,20},{20,24},{24,28},{1,5},{5,9},{9,... | collective-permute-start | bytes 786440 | tf_op jit(solution)/shard_map/ppermute | solution.py:20
  2.6 8.7 %collective-permute-start.1 = (f32[2,2,128,128]{3,2,1,0:T(8,128)}, f32[2,2,128,128]{3,2,1,0:T(8,128)S(1)}, u32[]{:S(2)}, u32[]{:S(2)}) collective-permute-start(f32[2,2,128,128]{3,2,1,0:T(8,128)} %param.10), channel_id=1, source_target_pairs={{4,0},{8,4},{12,8},{16,12},{20,16},{24,20},{28,24},{5,1},{9,5},{13... | collective-permute-start | bytes 786440 | tf_op jit(solution)/shard_map/ppermute | solution.py:20
  11.3 20.1 %collective-permute-start.3 = (f32[2,2,384,128]{3,2,1,0:T(8,128)S(1)}, f32[2,2,384,128]{3,2,1,0:T(8,128)S(1)}, u32[]{:S(2)}, u32[]{:S(2)}) collective-permute-start(f32[2,2,384,128]{3,2,1,0:T(8,128)S(1)} %constant_dynamic-update-slice_fusion), channel_id=1, source_target_pairs={{1,0},{2,1},{3,2},{5,4},{6,5},{7,6},{9,8},{10,9},{11,10},{13,12},{... | collective-permute-start | bytes 2359304 | tf_op jit(solution)/shard_map/ppermute | solution.py:20
  13.7 21.8 %collective-permute-start.2 = (f32[2,2,384,128]{3,2,1,0:T(8,128)S(1)}, f32[2,2,384,128]{3,2,1,0:T(8,128)S(1)}, u32[]{:S(2)}, u32[]{:S(2)}) collective-permute-start(f32[2,2,384,128]{3,2,1,0:T(8,128)S(1)} %constant_dynamic-update-slice_fusion), channel_id=1, source_target_pairs={{0,1},{1,2},{2,3},{4,5},{5,6},{6,7},{8,9},{9,10},{10,11},{12,13},{... | collective-permute-start | bytes 2359304 | tf_op jit(solution)/shard_map/ppermute | solution.py:20
  17.0 20.1 %copy-start = (bf16[2,256,256]{2,1,0:T(8,128)(2,1)S(1)}, bf16[2,256,256]{2,1,0:T(8,128)(2,1)}, u32[]{:S(2)}) copy-start(bf16[2,256,256]{2,1,0:T(8,128)(2,1)} %probe.1) | copy-start | bytes 786436
  17.0 20.1 %copy-start.1 = (bf16[1,1,2,256,256]{4,3,2,1,0:T(8,128)(2,1)S(1)}, bf16[1,1,2,256,256]{4,3,2,1,0:T(8,128)(2,1)}, u32[]{:S(2)}) copy-start(bf16[1,1,2,256,256]{4,3,2,1,0:T(8,128)(2,1)} %param.13) | copy-start | bytes 786436
  17.1 20.1 %copy-start.2 = (s32[1,1,2]{2,1,0:T(1,128)S(1)}, s32[1,1,2]{2,1,0:T(1,128)}, u32[]{:S(2)}) copy-start(s32[1,1,2]{2,1,0:T(1,128)} %param.15) | copy-start | bytes 28
  17.1 20.1 %copy-start.3 = (bf16[512,512]{1,0:T(8,128)(2,1)S(1)}, bf16[512,512]{1,0:T(8,128)(2,1)}, u32[]{:S(2)}) copy-start(bf16[512,512]{1,0:T(8,128)(2,1)} %constant.112.clone.fh) | copy-start | bytes 1572868
  17.1 20.1 %copy-start.4 = (bf16[512,512]{1,0:T(8,128)(2,1)S(1)}, bf16[512,512]{1,0:T(8,128)(2,1)}, u32[]{:S(2)}) copy-start(bf16[512,512]{1,0:T(8,128)(2,1)} %constant.113.clone.fl) | copy-start | bytes 1572868
  17.1 20.1 %copy-start.5 = (bf16[512,512]{1,0:T(8,128)(2,1)S(1)}, bf16[512,512]{1,0:T(8,128)(2,1)}, u32[]{:S(2)}) copy-start(bf16[512,512]{1,0:T(8,128)(2,1)} %constant.114.clone.ih) | copy-start | bytes 1572868
  17.1 20.1 %copy-start.6 = (bf16[512,512]{1,0:T(8,128)(2,1)S(1)}, bf16[512,512]{1,0:T(8,128)(2,1)}, u32[]{:S(2)}) copy-start(bf16[512,512]{1,0:T(8,128)(2,1)} %constant.115.clone.il) | copy-start | bytes 1572868
  61.8 5.0 %collective-permute-start.8 = (f32[2,2,2,32,256]{4,3,2,1,0:T(8,128)S(1)}, f32[2,2,2,32,256]{4,3,2,1,0:T(8,128)S(1)}, u32[]{:S(2)}, u32[]{:S(2)}) collective-permute-start(f32[2,2,2,32,256]{4,3,2,1,0:T(8,128)S(1)} %dynamic-slice_bitcast_fusion), channel_id=1, source_target_pairs={{0,4},{4,0},{8,12},{12,8},{16,20},{20,16},{24,28},{28,24},{1,5},{5... | collective-permute-start | bytes 786440 | tf_op jit(solution)/shard_map/ppermute | solution.py:58
  63.2 20.1 %collective-permute-start.5 = (f32[2,2,384,128]{3,2,1,0:T(8,128)}, f32[2,2,384,128]{3,2,1,0:T(8,128)S(1)}, u32[]{:S(2)}, u32[]{:S(2)}) collective-permute-start(f32[2,2,384,128]{3,2,1,0:T(8,128)} %get-tuple-element.7), channel_id=1, source_target_pairs={{1,0},{2,1},{3,2},{5,4},{6,5},{7,6},{9,8},{10,9},{11,10},{13,12},{... | collective-permute-start | bytes 2359304 | tf_op jit(solution)/shard_map/ppermute | solution.py:20
  65.5 21.9 %collective-permute-start.4 = (f32[2,2,384,128]{3,2,1,0:T(8,128)}, f32[2,2,384,128]{3,2,1,0:T(8,128)}, u32[]{:S(2)}, u32[]{:S(2)}) collective-permute-start(f32[2,2,384,128]{3,2,1,0:T(8,128)} %get-tuple-element.6), channel_id=1, source_target_pairs={{0,1},{1,2},{2,3},{4,5},{5,6},{6,7},{8,9},{9,10},{10,11},{12,13},{... | collective-permute-start | bytes 2359304 | tf_op jit(solution)/shard_map/ppermute | solution.py:20
  67.6 5.8 %collective-permute-start.9 = (f32[2,2,32,256]{3,2,0,1:T(8,128)}, f32[2,2,32,256]{3,2,0,1:T(8,128)S(1)}, u32[]{:S(2)}, u32[]{:S(2)}) collective-permute-start(f32[2,2,32,256]{3,2,0,1:T(8,128)} %bitcast.27), channel_id=1, source_target_pairs={{0,8},{4,12},{8,0},{12,4},{16,24},{20,28},{24,16},{28,20},{1,9},{5... | collective-permute-start | bytes 393224 | tf_op jit(solution)/shard_map/ppermute | solution.py:58
  73.5 4.3 %collective-permute-start.10 = (f32[2,32,256]{2,1,0:T(8,128)S(1)}, f32[2,32,256]{2,1,0:T(8,128)S(1)}, u32[]{:S(2)}, u32[]{:S(2)}) collective-permute-start(f32[2,32,256]{2,1,0:T(8,128)S(1)} %dynamic-slice_bitcast_fusion.1), channel_id=1, source_target_pairs={{0,16},{4,20},{8,24},{12,28},{16,0},{20,4},{24,8},{28,12},{1,17},{... | collective-permute-start | bytes 196616 | tf_op jit(solution)/shard_map/ppermute | solution.py:58
  83.2 0.9 copy-start.7
  88.9 15.0 %collective-permute-start.7 = (f32[2,2,128,128]{3,2,1,0:T(8,128)S(1)}, f32[2,2,128,128]{3,2,1,0:T(8,128)S(1)}, u32[]{:S(2)}, u32[]{:S(2)}) collective-permute-start(f32[2,2,128,128]{3,2,1,0:T(8,128)S(1)} %get-tuple-element.9), channel_id=1, source_target_pairs={{4,0},{8,4},{12,8},{16,12},{20,16},{24,20},{28,24},{5,1},{9,5},{13... | collective-permute-start | bytes 786440 | tf_op jit(solution)/shard_map/ppermute | solution.py:20
  90.9 13.0 %collective-permute-start.6 = (f32[2,2,128,128]{3,2,1,0:T(8,128)S(1)}, f32[2,2,128,128]{3,2,1,0:T(8,128)S(1)}, u32[]{:S(2)}, u32[]{:S(2)}) collective-permute-start(f32[2,2,128,128]{3,2,1,0:T(8,128)S(1)} %get-tuple-element.8), channel_id=1, source_target_pairs={{0,4},{4,8},{8,12},{12,16},{16,20},{20,24},{24,28},{1,5},{5,9},{9,... | collective-permute-start | bytes 786440 | tf_op jit(solution)/shard_map/ppermute | solution.py:20
  93.4 4.7 %collective-permute-start.11 = (f32[2,32,2,64]{3,2,1,0:T(2,128)S(1)}, f32[2,32,2,64]{3,2,1,0:T(2,128)S(1)}, u32[]{:S(2)}, u32[]{:S(2)}) collective-permute-start(f32[2,32,2,64]{3,2,1,0:T(2,128)S(1)} %bitcast.34), channel_id=1, source_target_pairs={{0,1},{1,0},{2,3},{3,2},{4,5},{5,4},{6,7},{7,6},{8,9},{9,8},{10,11... | collective-permute-start | bytes 98312 | tf_op jit(solution)/shard_map/ppermute | solution.py:58
  98.2 5.1 %collective-permute-start.12 = (f32[2,32,64]{2,1,0:T(8,128)S(1)}, f32[2,32,64]{2,1,0:T(8,128)S(1)}, u32[]{:S(2)}, u32[]{:S(2)}) collective-permute-start(f32[2,32,64]{2,1,0:T(8,128)S(1)} %bitcast.35), channel_id=1, source_target_pairs={{0,2},{1,3},{2,0},{3,1},{4,6},{5,7},{6,4},{7,5},{8,10},{9,11},{10,... | collective-permute-start | bytes 49160 | tf_op jit(solution)/shard_map/ppermute | solution.py:58

commit v2 on v1

v2 whole, which is shorter than its diff:
```python
import math

import jax
import jax.numpy as jnp
import ml_dtypes
import numpy as np
from jax import lax
from jax.experimental import pallas as pl
from jax.experimental.pallas import tpu as pltpu
from jax.sharding import PartitionSpec as P

MESH = pl.DeviceIdType.MESH


def split(value):
    high = value.astype(jnp.bfloat16)
    low = (value - high.astype(jnp.float32)).astype(jnp.bfloat16)
    return high, low


def tables(width):
    index = np.arange(width)
    angles = (np.outer(index, index) % width) * (2.0 * math.pi / width)
    cosine = np.cos(angles) / math.sqrt(width)
    sine = np.sin(angles) / math.sqrt(width)
    out = []
    for orient in (-1.0, 1.0):
        block = np.block([[cosine, orient * sine], [-orient * sine, cosine]]).astype(np.float32)
        high = block.astype(ml_dtypes.bfloat16)
        low = (block - high.astype(np.float32)).astype(ml_dtypes.bfloat16)
        out += [high, low]
    return out


def dot(left, right):
    return jnp.dot(left, right, preferred_element_type=jnp.float32)


def make_transform(forward, inverse, width):
    def transform(values, orient):
        first, second = (forward, inverse) if orient < 0 else (inverse, forward)
        high, low = split(jnp.concatenate(values, axis=1))
        table = first[0][...]
        once = dot(high, table) + dot(low, table) + dot(high, first[1][...])
        high, low = split(jnp.concatenate([once[:, :width], once[:, width:]], axis=0))
        table = second[0][...]
        twice = dot(table, high) + dot(table, low) + dot(second[1][...], high)
        return (twice[:width], twice[width:])

    return transform


def product(left, right):
    return (left[0] * right[0] - left[1] * right[1], left[0] * right[1] + left[1] * right[0])


def conjugate(values):
    return (values[0], -values[1])


def kernel(
    centres, live, tile, probe, phase, intensity, tables_hbm, out, probe_out,
    table, ext, acc, field_one, upstream_one, adjoint_zero, prop,
    first_cols, first_rows, last_in, mid_cols, mid_rows,
    terms, arrived, blocks, blocks_in, table_sem,
    halo_send, halo_recv, fold_send, fold_recv, sum_send, sum_recv,
):
    slices, slot_count = tile.shape[0], intensity.shape[0]
    width = probe.shape[1]
    half = width // 2
    size = tile.shape[2] + width
    sizes = {"row": lax.axis_size("row"), "col": lax.axis_size("col")}
    at = {"row": lax.axis_index("row"), "col": lax.axis_index("col")}
    bits = {name: sizes[name].bit_length() - 1 for name in sizes}
    steps = [("row", bit) for bit in range(bits["row"])] + [("col", bit) for bit in range(bits["col"])]
    first, middle, last = pl.ds(0, half), pl.ds(half, half), pl.ds(2 * half, half)
    every = pl.ds(0, size)

    def has(axis, delta):
        return at[axis] > 0 if delta < 0 else at[axis] < sizes[axis] - 1

    def partner(axis, bit):
        odd = lax.rem(at[axis] // (1 << bit), 2)
        return odd, at[axis] + (1 - 2 * odd) * (1 << bit)

    barrier = pltpu.get_barrier_semaphore()
    count = 0
    for axis in ("row", "col"):
        for delta in (-1, 1):
            @pl.when(has(axis, delta))
            def _(axis=axis, delta=delta):
                pl.semaphore_signal(barrier, inc=1, device_id={axis: at[axis] + delta}, device_id_type=MESH)
            count = count + jnp.where(has(axis, delta), 1, 0)
    for axis, bit in steps:
        if bit > 0:
            pl.semaphore_signal(barrier, inc=1, device_id={axis: partner(axis, bit)[1]}, device_id_type=MESH)
            count = count + 1
    pl.semaphore_wait(barrier, count)

    class Shift:
        def __init__(self, src, dst, send, recv, axis, delta):
            n = sizes[axis]
            self.copy = pltpu.make_async_remote_copy(
                src_ref=src, dst_ref=dst, send_sem=send, recv_sem=recv,
                device_id={axis: lax.rem(at[axis] + delta + n, n)}, device_id_type=MESH,
            )
            self.target, self.source = has(axis, delta), has(axis, -delta)

        def start(self):
            pl.when(self.target)(lambda: self.copy.start())

        def wait_recv(self):
            pl.when(self.source)(lambda: self.copy.wait_recv())

        def wait_send(self):
            pl.when(self.target)(lambda: self.copy.wait_send())

    def halo(s, part):
        copies = []
        for side, delta in enumerate((1, -1)):
            place = first if delta > 0 else last
            for c in range(2):
                if c == 0 and part == 0:
                    src, dst, axis = tile.at[s, c], ext[s][c].at[place, middle], "row"
                elif c == 0:
                    src, dst, axis = ext[s][c].at[every, middle], ext[s][c].at[every, place], "col"
                elif part == 0:
                    src, dst, axis = tile.at[s, c], ext[s][c].at[middle, place], "col"
                else:
                    src, dst, axis = ext[s][c].at[middle, every], ext[s][c].at[place, every], "row"
                sem = ((s * 2 + part) * 2 + c) * 2 + side
                copies.append(Shift(src, dst, halo_send.at[sem], halo_recv.at[sem], axis, delta))
        return copies

    def folding(s, part):
        copies = []
        for side, delta in enumerate((1, -1)):
            place = last if delta > 0 else first
            for c in range(2):
                if c == 0 and part == 0:
                    src, dst, axis = acc[s][c].at[every, place], first_cols[s][side], "col"
                elif c == 0:
                    src, dst, axis = mid_cols[s].at[place, :], last_in[s][c][side], "row"
                elif part == 0:
                    src, dst, axis = acc[s][c].at[place, every], first_rows[s][side], "row"
                else:
                    src, dst, axis = mid_rows[s].at[:, place], last_in[s][c][side], "col"
                sem = ((s * 2 + part) * 2 + c) * 2 + side
                copies.append(Shift(src, dst, fold_send.at[sem], fold_recv.at[sem], axis, delta))
        return copies

    def start_all(copies):
        for copy in copies:
            copy.start()
        sent.extend(copies)

    def arrive_all(copies):
        for copy in copies:
            copy.wait_recv()

    sent = []
    halos = [[halo(s, part) for part in range(2)] for s in range(slices)]
    folds = [[folding(s, part) for part in range(2)] for s in range(slices)]
    for s in range(slices):
        start_all(halos[s][0])
    loads = [pltpu.make_async_copy(tables_hbm.at[k], table.at[k], table_sem.at[k]) for k in range(4)]
    for load in loads:
        load.start()

    for s in range(slices):
        for c in range(2):
            ext[s][c][middle, middle] = tile[s, c]
        for side, delta in enumerate((1, -1)):
            place = first if delta > 0 else last

            @pl.when(jnp.logical_not(has("row", -delta)))
            def _(s=s, side=side, place=place):
                ext[s][0][place, middle] = jnp.zeros((half, half), jnp.float32)
                ext[s][1][place, every] = jnp.zeros((half, size), jnp.float32)
                first_rows[s][side][...] = jnp.zeros((half, size), jnp.float32)
                last_in[s][0][side][...] = jnp.zeros((half, half), jnp.float32)

            @pl.when(jnp.logical_not(has("col", -delta)))
            def _(s=s, side=side, place=place):
                ext[s][1][middle, place] = jnp.zeros((half, half), jnp.float32)
                ext[s][0][every, place] = jnp.zeros((size, half), jnp.float32)
                first_cols[s][side][...] = jnp.zeros((size, half), jnp.float32)
                last_in[s][1][side][...] = jnp.zeros((half, half), jnp.float32)

    for s in range(slices):
        arrive_all(halos[s][0])
        start_all(halos[s][1])

    angles = phase[...].astype(jnp.float32)
    prop[0] = jnp.cos(angles)
    prop[1] = jnp.sin(angles)
    for load in loads:
        load.wait()
    arrive_all(halos[0][1])

    transform = make_transform(
        (table.at[0], table.at[1]), (table.at[2], table.at[3]), width
    )

    def start_of(slot):
        row = centres[slot, 0] - at["row"] * tile.shape[2]
        return row, centres[slot, 1] - at["col"] * tile.shape[3]

    def window(s, slot):
        row, col = start_of(slot)
        parts = []
        for c in range(2):
            band = pltpu.roll(ext[s][c][...], lax.rem(size - row, size), 0)[:width]
            parts.append(pltpu.roll(band, lax.rem(size - col, size), 1)[:, :width])
        return tuple(parts)

    def place_term(s, slot, values):
        row, col = start_of(slot)
        for c in range(2):
            wide = jnp.concatenate([values[c], jnp.zeros((width, size - width), jnp.float32)], axis=1)
            wide = pltpu.roll(wide, col, 1)
            tall = jnp.concatenate([wide, jnp.zeros((size - width, size), jnp.float32)], axis=0)
            acc[s][c][...] += pltpu.roll(tall, row, 0)

    def entering_zero():
        return (probe[0].astype(jnp.float32), probe[1].astype(jnp.float32))

    def pair(ref, slot):
        return (ref[slot, 0], ref[slot, 1])

    def keep(ref, slot, values):
        ref[slot, 0] = values[0]
        ref[slot, 1] = values[1]

    for s in range(slices):
        for c in range(2):
            acc[s][c][...] = jnp.zeros((size, size), jnp.float32)
    terms[0][...] = jnp.zeros(terms[0].shape, jnp.float32)

    def forward(slot, carry):
        spectrum = transform(product(entering_zero(), window(0, slot)), -1.0)
        keep(field_one, slot, transform(product(spectrum, (prop[0], prop[1])), 1.0))
        return carry

    lax.fori_loop(0, slot_count, forward, 0)
    arrive_all(halos[1][1])

    def turn(slot, carry):
        layer = window(1, slot)
        field = pair(field_one, slot)
        spectrum = transform(product(field, layer), -1.0)
        measured = intensity[slot].astype(jnp.float32)
        weight = jnp.where(live[slot] >= 0, 1.0, 0.0).astype(jnp.float32)
        misfit = weight * (spectrum[0] * spectrum[0] + spectrum[1] * spectrum[1] - measured)
        adjoint = transform((misfit * spectrum[0], misfit * spectrum[1]), 1.0)
        place_term(1, slot, product(conjugate(field), adjoint))
        keep(upstream_one, slot, product(conjugate(layer), adjoint))
        return carry

    lax.fori_loop(0, slot_count, turn, 0)
    start_all(folds[1][0])

    def fold_middle(s):
        arrive_all(folds[s][0])
        mid_cols[s][...] = acc[s][0][every, middle] + first_cols[s][0][...] + first_cols[s][1][...]
        mid_rows[s][...] = acc[s][1][middle, every] + first_rows[s][0][...] + first_rows[s][1][...]
        start_all(folds[s][1])

    def fold_end(s):
        arrive_all(folds[s][1])
        out[s, 0] = mid_cols[s][middle, :] + last_in[s][0][0][...] + last_in[s][0][1][...]
        out[s, 1] = mid_rows[s][:, middle] + last_in[s][1][0][...] + last_in[s][1][1][...]

    def back(slot, carry):
        spectrum = transform(pair(upstream_one, slot), -1.0)
        adjoint = transform(product(spectrum, conjugate((prop[0], prop[1]))), 1.0)
        keep(adjoint_zero, slot, adjoint)
        upstream = product(conjugate(window(0, slot)), adjoint)
        for c in range(2):
            terms[0][c] += upstream[c].reshape(terms[0].shape[1:])
        pl.when(slot == 0)(lambda: fold_middle(1))
        return carry

    lax.fori_loop(0, slot_count, back, 0)

    def halving(step):
        axis, bit = steps[step]
        odd, other = partner(axis, bit)
        held = terms[step] if axis == "row" else blocks[bit]
        landing = arrived[step] if axis == "row" else blocks_in[bit]
        copy = pltpu.make_async_remote_copy(
            src_ref=held.at[:, :, 1 - odd], dst_ref=landing,
            send_sem=sum_send.at[step], recv_sem=sum_recv.at[step],
            device_id={axis: other}, device_id_type=MESH,
        )
        return copy, held, landing, odd

    halvings = [halving(step) for step in range(len(steps))]

    def sum_next(step):
        copy, held, landing, odd = halvings[step]
        copy.wait()
        total = held[:, :, odd] + landing[...]
        if step + 1 == len(steps):
            probe_out[...] = total[:, 0, :, : probe_out.shape[2]]
            return
        if step + 1 < bits["row"]:
            terms[step + 1][...] = total.reshape(terms[step + 1].shape)
        elif step + 1 == bits["row"]:
            span = probe_out.shape[2]
            for j in range(sizes["col"]):
                blocks[0][:, j // 2, j % 2, :, :span] = total[:, 0, :, j * span : (j + 1) * span]
        else:
            following = blocks[step + 1 - bits["row"]]
            following[...] = total.reshape(following.shape)
        halvings[step + 1][0].start()

    if blocks[0].shape[-1] > probe_out.shape[2]:
        blocks[0][...] = jnp.zeros(blocks[0].shape, jnp.float32)
    halvings[0][0].start()

    def place_zero(slot, carry):
        place_term(0, slot, product(conjugate(entering_zero()), pair(adjoint_zero, slot)))
        return carry

    lax.fori_loop(0, slot_count, place_zero, 0)
    start_all(folds[0][0])
    sum_next(0)
    fold_end(1)
    sum_next(1)
    fold_middle(0)
    for step in range(2, len(steps) - 1):
        sum_next(step)
    fold_end(0)
    sum_next(len(steps) - 1)
    for copy in sent:
        copy.wait_send()


def per_device(object_slices, probe_wave, propagator_phase, intensity, centres, batch_order):
    slices = object_slices.shape[0]
    half = object_slices.shape[2]
    width = probe_wave.shape[1]
    size = half + width
    slot_count = centres.shape[2]
    rows, cols = lax.axis_size("row"), lax.axis_size("col")
    block_rows, block_cols = width // rows, width // cols
    lanes = max(block_cols, 128)
    row_bits, col_bits = rows.bit_length() - 1, cols.bit_length() - 1
    smem = pl.BlockSpec(memory_space=pltpu.SMEM)
    vmem = pl.BlockSpec(memory_space=pltpu.VMEM)

    def floats(*shape):
        return pltpu.VMEM(shape, jnp.float32)

    def sems(count):
        return pltpu.SemaphoreType.DMA((count,))

    slot_fields = floats(slot_count, 2, width, width)
    scratch = [
        pltpu.VMEM((4, 2 * width, 2 * width), jnp.bfloat16),
        [[floats(size, size)] * 2] * slices,
        [[floats(size, size)] * 2] * slices,
        slot_fields,
        slot_fields,
        slot_fields,
        floats(2, width, width),
        [[floats(size, half)] * 2] * slices,
        [[floats(half, size)] * 2] * slices,
        [[[floats(half, half)] * 2] * 2] * slices,
        [floats(size, half)] * slices,
        [floats(half, size)] * slices,
        [floats(2, rows >> (k + 1), 2, block_rows, width) for k in range(row_bits)],
        [floats(2, rows >> (k + 1), block_rows, width) for k in range(row_bits)],
        [floats(2, cols >> (k + 1), 2, block_rows, lanes) for k in range(col_bits)],
        [floats(2, cols >> (k + 1), block_rows, lanes) for k in range(col_bits)],
        sems(4),
        sems(8 * slices),
        sems(8 * slices),
        sems(8 * slices),
        sems(8 * slices),
        sems(row_bits + col_bits),
        sems(row_bits + col_bits),
    ]
    flops = slot_count * 6 * 2 * 3 * 2 * width * 4 * width * width
    return pl.pallas_call(
        kernel,
        out_shape=(
            jax.ShapeDtypeStruct(object_slices.shape, jnp.float32),
            jax.ShapeDtypeStruct((2, block_rows, block_cols), jnp.float32),
        ),
        in_specs=[smem] * 2 + [vmem] * 4 + [pl.BlockSpec(memory_space=pl.ANY)],
        out_specs=(vmem, vmem),
        scratch_shapes=scratch,
        compiler_params=pltpu.CompilerParams(
            vmem_limit_bytes=52 * 2**20, collective_id=0, has_side_effects=True
        ),
        cost_estimate=pl.CostEstimate(flops=flops, bytes_accessed=8 * 2**20, transcendentals=0),
    )(
        centres[0, 0], batch_order[0, 0], object_slices, probe_wave, propagator_phase,
        intensity[0, 0], jnp.asarray(np.stack(tables(width))),
    )


def solution(mesh):
    placed = (
        P(None, None, "row", "col"),
        P(),
        P(),
        P("row", "col", None, None, None),
        P("row", "col", None, None),
        P("row", "col", None),
    )
    return jax.shard_map(
        per_device,
        mesh=mesh,
        in_specs=placed,
        out_specs=(P(None, None, "row", "col"), P(None, "row", "col")),
        check_vma=False,
    )
```

time: 105 us -> 67.7 us (0.64)
  the two profiles are of different devices: /device:TPU:28 before, /device:TPU:0 now
where the time goes in v2:
time: 67.7 us; the launch traced here: 67.4 us
  Pallas kernels  60.3 us (89%)
  local copies, waits for them, and re-layouts  6.4 us (9%)
    pallas_call x1, Pallas kernels, per_device(): pl.pallas_call(kernel, out_shape=(jax.ShapeDtypeStruct(object_slices.shap...  60.3 us
    unnamed x14, local copies, waits for them, and re-layouts  6.4 us

profile of v2, /device:TPU:0, one launch (start us, length us, event | category | flops | bytes accessed | tf_op | source)
XLA Modules:
  0.0 67.4 jit_solution(7630134246926079020)
XLA Ops:
  0.6 0.0 copy-start
  0.6 0.9 %copy-done = f32[2,2,128,128]{3,2,1,0:T(8,128)S(1)} copy-done((f32[2,2,128,128]{3,2,1,0:T(8,128)S(1)}, f32[2,2,128,128]{3,2,1,0:T(8,128)}, u32[]{:S(2)}) %copy-start) | copy-done | bytes 262168
  1.6 0.0 copy-start.1
  1.6 0.9 %copy-done.1 = bf16[2,256,256]{2,1,0:T(8,128)(2,1)S(1)} copy-done((bf16[2,256,256]{2,1,0:T(8,128)(2,1)S(1)}, bf16[2,256,256]{2,1,0:T(8,128)(2,1)}, u32[]{:S(2)}) %copy-start.1) | copy-done | bytes 262168
  2.5 0.0 copy-start.2
  2.5 0.9 %copy-done.2 = bf16[1,1,2,256,256]{4,3,2,1,0:T(8,128)(2,1)S(1)} copy-done((bf16[1,1,2,256,256]{4,3,2,1,0:T(8,128)(2,1)S(1)}, bf16[1,1,2,256,256]{4,3,2,1,0:T(8,128)(2,1)}, u32[]{:S(2)}) %copy-start.2) | copy-done | bytes 262168
  3.5 0.0 copy-start.3
  3.5 0.9 %copy-done.3 = bf16[256,256]{1,0:T(8,128)(2,1)S(1)} copy-done((bf16[256,256]{1,0:T(8,128)(2,1)S(1)}, bf16[256,256]{1,0:T(8,128)(2,1)}, u32[]{:S(2)}) %copy-start.3) | copy-done | bytes 131096
  4.4 0.0 copy-start.4
  4.4 0.7 %copy-done.4 = s32[1,1,2,2]{3,2,1,0:T(2,128)S(1)} copy-done((s32[1,1,2,2]{3,2,1,0:T(2,128)S(1)}, s32[1,1,2,2]{3,2,1,0:T(2,128)}, u32[]{:S(2)}) %copy-start.4) | copy-done | bytes 40
  5.1 0.0 copy-start.5
  5.1 0.7 copy-done.5
  5.7 60.3 %shard_map.86 = (f32[2,2,128,128]{3,2,1,0:T(8,128)S(1)}, f32[2,32,64]{2,1,0:T(8,128)S(1)}) custom-call(s32[2,2]{1,0:T(2,128)S(1)} %bitcast.4, s32[2]{0:T(128)S(1)} %bitcast.5, f32[2,2,128,128]{3,2,1,0:T(8,128)S(1)} %copy-done, bf16[2,256,256]{2,1,0:T(8,128)(2,1)S(1)} %copy-done.1, bf16[256,256]{1,0:T(8,128)(2,1)S(1)} %copy-done.3, ...), custom_call_target="tpu_custom_call" | custom-call | flops 9663676416 | bytes 8388608 | tf_op jit(solution)/shard_map/pallas_call | solution.py:386
  66.1 0.7 %copy.11 = f32[2,2,128,128]{3,2,1,0:T(8,128)} copy(f32[2,2,128,128]{3,2,1,0:T(8,128)S(1)} %get-tuple-element.4) | data formatting | bytes 524288
  66.8 0.6 copy.12
Async XLA Ops:
  0.6 1.0 %copy-start = (f32[2,2,128,128]{3,2,1,0:T(8,128)S(1)}, f32[2,2,128,128]{3,2,1,0:T(8,128)}, u32[]{:S(2)}) copy-start(f32[2,2,128,128]{3,2,1,0:T(8,128)} %tile.1) | copy-start | bytes 786436
  1.6 0.9 %copy-start.1 = (bf16[2,256,256]{2,1,0:T(8,128)(2,1)S(1)}, bf16[2,256,256]{2,1,0:T(8,128)(2,1)}, u32[]{:S(2)}) copy-start(bf16[2,256,256]{2,1,0:T(8,128)(2,1)} %probe.1) | copy-start | bytes 786436
  2.5 0.9 %copy-start.2 = (bf16[1,1,2,256,256]{4,3,2,1,0:T(8,128)(2,1)S(1)}, bf16[1,1,2,256,256]{4,3,2,1,0:T(8,128)(2,1)}, u32[]{:S(2)}) copy-start(bf16[1,1,2,256,256]{4,3,2,1,0:T(8,128)(2,1)} %param.10) | copy-start | bytes 786436
  3.5 0.9 %copy-start.3 = (bf16[256,256]{1,0:T(8,128)(2,1)S(1)}, bf16[256,256]{1,0:T(8,128)(2,1)}, u32[]{:S(2)}) copy-start(bf16[256,256]{1,0:T(8,128)(2,1)} %phase.1) | copy-start | bytes 393220
  4.4 0.7 %copy-start.4 = (s32[1,1,2,2]{3,2,1,0:T(2,128)S(1)}, s32[1,1,2,2]{3,2,1,0:T(2,128)}, u32[]{:S(2)}) copy-start(s32[1,1,2,2]{3,2,1,0:T(2,128)} %param.11) | copy-start | bytes 52
  5.1 0.7 copy-start.5

commit v3 on v2

--- a/solution.py
+++ b/solution.py
@@ -19,33 +19,84 @@
 
 
 def tables(width):
-    index = np.arange(width)
-    angles = (np.outer(index, index) % width) * (2.0 * math.pi / width)
+    half = width // 2
+    index = np.arange(half)
+    angles = (np.outer(index, index) % half) * (2.0 * math.pi / half)
     cosine = np.cos(angles) / math.sqrt(width)
     sine = np.sin(angles) / math.sqrt(width)
     out = []
     for orient in (-1.0, 1.0):
         block = np.block([[cosine, orient * sine], [-orient * sine, cosine]]).astype(np.float32)
         high = block.astype(ml_dtypes.bfloat16)
-        low = (block - high.astype(np.float32)).astype(ml_dtypes.bfloat16)
-        out += [high, low]
-    return out
+        out += [high, (block - high.astype(np.float32)).astype(ml_dtypes.bfloat16)]
+    order = np.eye(width)[np.concatenate([np.arange(0, width, 2), np.arange(1, width, 2)])]
+    out += [order.astype(ml_dtypes.bfloat16), order.T.astype(ml_dtypes.bfloat16)]
+    turns = np.zeros((2, half + 8, width), np.float32)
+    for part, values in enumerate((np.cos(index * 2.0 * math.pi / width), np.sin(index * 2.0 * math.pi / width))):
+        turns[part, :half] = values[:, None]
+        turns[part, half, :half] = values
+    return np.stack(out), turns
 
 
 def dot(left, right):
     return jnp.dot(left, right, preferred_element_type=jnp.float32)
 
 
-def make_transform(forward, inverse, width):
+def make_transform(table, turns, width, count):
+    half = width // 2
+
+    def right_dot(value, at):
+        high, low = split(value)
+        return dot(high, table[at]) + dot(low, table[at]) + dot(high, table[at + 1])
+
+    def left_dot(value, at):
+        high, low = split(value)
+        return dot(table[at], high) + dot(table[at], low) + dot(table[at + 1], high)
+
+    def along_cols(values, orient):
+        re, im = values
+        rows = re.shape[0]
+        cosine, sine = (turns[0, half : half + 1, :half], turns[1, half : half + 1, :half])
+        one, two = ((re[:, :half], im[:, :half]), (re[:, half:], im[:, half:]))
+        if orient < 0:
+            one, two = (one[0] + two[0], one[1] + two[1]), (one[0] - two[0], one[1] - two[1])
+            two = product(two, (cosine, -sine))
+        stacked = jnp.concatenate([jnp.concatenate(one, axis=1), jnp.concatenate(two, axis=1)], axis=0)
+        result = right_dot(stacked, 0 if orient < 0 else 2)
+        one = (result[:rows, :half], result[:rows, half:])
+        two = (result[rows:, :half], result[rows:, half:])
+        if orient > 0:
+            two = product(two, (cosine, sine))
+            one, two = (one[0] + two[0], one[1] + two[1]), (one[0] - two[0], one[1] - two[1])
+        return tuple(jnp.concatenate([one[c], two[c]], axis=1) for c in range(2))
+
+    def along_rows(values, orient):
+        re, im = values
+        cosine, sine = (turns[0, :half], turns[1, :half])
+        pieces = []
+        for slot in range(count):
+            top, mid, end = (slot * width, slot * width + half, (slot + 1) * width)
+            one, two = ((re[top:mid], im[top:mid]), (re[mid:end], im[mid:end]))
+            if orient < 0:
+                one, two = (one[0] + two[0], one[1] + two[1]), (one[0] - two[0], one[1] - two[1])
+                two = product(two, (cosine, -sine))
+            pieces += [jnp.concatenate(one, axis=0), jnp.concatenate(two, axis=0)]
+        result = left_dot(jnp.concatenate(pieces, axis=1), 2 if orient < 0 else 0)
+        parts = ([], [])
+        for slot in range(count):
+            left = 2 * slot * width
+            one = (result[:half, left : left + width], result[half:, left : left + width])
+            left += width
+            two = (result[:half, left : left + width], result[half:, left : left + width])
+            if orient > 0:
+                two = product(two, (cosine, sine))
+                one, two = (one[0] + two[0], one[1] + two[1]), (one[0] - two[0], one[1] - two[1])
+            for c in range(2):
+                parts[c].extend([one[c], two[c]])
+        return tuple(jnp.concatenate(parts[c], axis=0) for c in range(2))
+
     def transform(values, orient):
-        first, second = (forward, inverse) if orient < 0 else (inverse, forward)
-        high, low = split(jnp.concatenate(values, axis=1))
-        table = first[0][...]
-        once = dot(high, table) + dot(low, table) + dot(high, first[1][...])
-        high, low = split(jnp.concatenate([once[:, :width], once[:, width:]], axis=0))
-        table = second[0][...]
-        twice = dot(table, high) + dot(table, low) + dot(second[1][...], high)
-        return (twice[:width], twice[width:])
+        return along_rows(along_cols(values, orient), orient)
 
     return transform
 
@@ -59,8 +110,8 @@
 
 
 def kernel(
-    centres, live, tile, probe, phase, intensity, tables_hbm, out, probe_out,
-    table, ext, acc, field_one, upstream_one, adjoint_zero, prop,
+    centres, live, tile, probe_hbm, phase_hbm, intensity_hbm, tables_hbm, turns_hbm, out, probe_out,
+    probe, phase, intensity, table, turns, ext, acc, layer_zero, field_one, upstream_one, prop, measured,
     first_cols, first_rows, last_in, mid_cols, mid_rows,
     terms, arrived, blocks, blocks_in, table_sem,
     halo_send, halo_recv, fold_send, fold_recv, sum_send, sum_recv,
@@ -163,13 +214,15 @@
     folds = [[folding(s, part) for part in range(2)] for s in range(slices)]
     for s in range(slices):
         start_all(halos[s][0])
-    loads = [pltpu.make_async_copy(tables_hbm.at[k], table.at[k], table_sem.at[k]) for k in range(4)]
+    moves = [(tables_hbm, table), (phase_hbm, phase), (intensity_hbm, intensity), (turns_hbm, turns), (probe_hbm, probe)]
+    moves += [(tile.at[s, c], ext[s][c].at[middle, middle]) for s in range(slices) for c in range(2)]
+    loads = [pltpu.make_async_copy(src, dst, table_sem.at[k]) for k, (src, dst) in enumerate(moves)]
     for load in loads:
         load.start()
 
     for s in range(slices):
         for c in range(2):
-            ext[s][c][middle, middle] = tile[s, c]
+            acc[s][c][...] = jnp.zeros((size, size), jnp.float32)
         for side, delta in enumerate((1, -1)):
             place = first if delta > 0 else last
 
@@ -187,20 +240,23 @@
                 first_cols[s][side][...] = jnp.zeros((size, half), jnp.float32)
                 last_in[s][1][side][...] = jnp.zeros((half, half), jnp.float32)
 
+    for load in loads:
+        load.wait()
     for s in range(slices):
         arrive_all(halos[s][0])
         start_all(halos[s][1])
 
-    angles = phase[...].astype(jnp.float32)
+    def reordered(values):
+        return dot(dot(table[4], values).astype(jnp.bfloat16), table[5])
+
+    angles = reordered(phase[...])
     prop[0] = jnp.cos(angles)
     prop[1] = jnp.sin(angles)
-    for load in loads:
-        load.wait()
+    for slot in range(slot_count):
+        measured[pl.ds(slot * width, width), :] = reordered(intensity[slot])
     arrive_all(halos[0][1])
 
-    transform = make_transform(
-        (table.at[0], table.at[1]), (table.at[2], table.at[3]), width
-    )
+    transform = make_transform(table, turns, width, slot_count)
 
     def start_of(slot):
         row = centres[slot, 0] - at["row"] * tile.shape[2]
@@ -222,42 +278,45 @@
             tall = jnp.concatenate([wide, jnp.zeros((size - width, size), jnp.float32)], axis=0)
             acc[s][c][...] += pltpu.roll(tall, row, 0)
 
+    def stack(pieces):
+        return tuple(jnp.concatenate([piece[c] for piece in pieces], axis=0) for c in range(2))
+
     def entering_zero():
-        return (probe[0].astype(jnp.float32), probe[1].astype(jnp.float32))
-
-    def pair(ref, slot):
-        return (ref[slot, 0], ref[slot, 1])
-
-    def keep(ref, slot, values):
-        ref[slot, 0] = values[0]
-        ref[slot, 1] = values[1]
-
-    for s in range(slices):
-        for c in range(2):
-            acc[s][c][...] = jnp.zeros((size, size), jnp.float32)
-    terms[0][...] = jnp.zeros(terms[0].shape, jnp.float32)
-
-    def forward(slot, carry):
-        spectrum = transform(product(entering_zero(), window(0, slot)), -1.0)
-        keep(field_one, slot, transform(product(spectrum, (prop[0], prop[1])), 1.0))
-        return carry
-
-    lax.fori_loop(0, slot_count, forward, 0)
+        return stack([(probe[0].astype(jnp.float32), probe[1].astype(jnp.float32))] * slot_count)
+
+    def pair(ref):
+        return (ref[0], ref[1])
+
+    def keep(ref, values):
+        ref[0] = values[0]
+        ref[1] = values[1]
+
+    def propagator():
+        return stack([pair(prop)] * slot_count)
+
+    def place_terms(s, values):
+        for slot in range(slot_count):
+            rows = slice(slot * width, (slot + 1) * width)
+            place_term(s, slot, (values[0][rows], values[1][rows]))
+
+    keep(layer_zero, stack([window(0, slot) for slot in range(slot_count)]))
+    spectrum = transform(product(entering_zero(), pair(layer_zero)), -1.0)
+    keep(field_one, transform(product(spectrum, propagator()), 1.0))
     arrive_all(halos[1][1])
 
-    def turn(slot, carry):
-        layer = window(1, slot)
-        field = pair(field_one, slot)
-        spectrum = transform(product(field, layer), -1.0)
-        measured = intensity[slot].astype(jnp.float32)
-        weight = jnp.where(live[slot] >= 0, 1.0, 0.0).astype(jnp.float32)
-        misfit = weight * (spectrum[0] * spectrum[0] + spectrum[1] * spectrum[1] - measured)
-        adjoint = transform((misfit * spectrum[0], misfit * spectrum[1]), 1.0)
-        place_term(1, slot, product(conjugate(field), adjoint))
-        keep(upstream_one, slot, product(conjugate(layer), adjoint))
-        return carry
-
-    lax.fori_loop(0, slot_count, turn, 0)
+    layer = stack([window(1, slot) for slot in range(slot_count)])
+    spectrum = transform(product(pair(field_one), layer), -1.0)
+    weights = jnp.concatenate(
+        [
+            jnp.full((width, width), jnp.where(live[slot] >= 0, 1.0, 0.0).astype(jnp.float32))
+            for slot in range(slot_count)
+        ],
+        axis=0,
+    )
+    misfit = weights * (spectrum[0] * spectrum[0] + spectrum[1] * spectrum[1] - measured[...])
+    adjoint = transform((misfit * spectrum[0], misfit * spectrum[1]), 1.0)
+    place_terms(1, product(conjugate(pair(field_one)), adjoint))
+    keep(upstream_one, product(conjugate(layer), adjoint))
     start_all(folds[1][0])
 
     def fold_middle(s):
@@ -271,17 +330,15 @@
         out[s, 0] = mid_cols[s][middle, :] + last_in[s][0][0][...] + last_in[s][0][1][...]
         out[s, 1] = mid_rows[s][:, middle] + last_in[s][1][0][...] + last_in[s][1][1][...]
 
-    def back(slot, carry):
-        spectrum = transform(pair(upstream_one, slot), -1.0)
-        adjoint = transform(product(spectrum, conjugate((prop[0], prop[1]))), 1.0)
-        keep(adjoint_zero, slot, adjoint)
-        upstream = product(conjugate(window(0, slot)), adjoint)
-        for c in range(2):
-            terms[0][c] += upstream[c].reshape(terms[0].shape[1:])
-        pl.when(slot == 0)(lambda: fold_middle(1))
-        return carry
-
-    lax.fori_loop(0, slot_count, back, 0)
+    spectrum = transform(pair(upstream_one), -1.0)
+    fold_middle(1)
+    adjoint = transform(product(spectrum, conjugate(propagator())), 1.0)
+    upstream = product(conjugate(pair(layer_zero)), adjoint)
+    for c in range(2):
+        total = upstream[c][:width]
+        for slot in range(1, slot_count):
+            total = total + upstream[c][slot * width : (slot + 1) * width]
+        terms[0][c] = total.reshape(terms[0].shape[1:])
 
     def halving(step):
         axis, bit = steps[step]
@@ -319,11 +376,7 @@
         blocks[0][...] = jnp.zeros(blocks[0].shape, jnp.float32)
     halvings[0][0].start()
 
-    def place_zero(slot, carry):
-        place_term(0, slot, product(conjugate(entering_zero()), pair(adjoint_zero, slot)))
-        return carry
-
-    lax.fori_loop(0, slot_count, place_zero, 0)
+    place_terms(0, product(conjugate(entering_zero()), adjoint))
     start_all(folds[0][0])
     sum_next(0)
     fold_end(1)
@@ -356,15 +409,21 @@
     def sems(count):
         return pltpu.SemaphoreType.DMA((count,))
 
-    slot_fields = floats(slot_count, 2, width, width)
+    slot_fields = floats(2, slot_count * width, width)
+    constants, twiddles = tables(width)
     scratch = [
-        pltpu.VMEM((4, 2 * width, 2 * width), jnp.bfloat16),
+        pltpu.VMEM(probe_wave.shape, probe_wave.dtype),
+        pltpu.VMEM(propagator_phase.shape, propagator_phase.dtype),
+        pltpu.VMEM(intensity.shape[2:], intensity.dtype),
+        pltpu.VMEM(constants.shape, jnp.bfloat16),
+        floats(*twiddles.shape),
         [[floats(size, size)] * 2] * slices,
         [[floats(size, size)] * 2] * slices,
         slot_fields,
         slot_fields,
         slot_fields,
         floats(2, width, width),
+        floats(slot_count * width, width),
         [[floats(size, half)] * 2] * slices,
         [[floats(half, size)] * 2] * slices,
         [[[floats(half, half)] * 2] * 2] * slices,
@@ -374,7 +433,7 @@
         [floats(2, rows >> (k + 1), block_rows, width) for k in range(row_bits)],
         [floats(2, cols >> (k + 1), 2, block_rows, lanes) for k in range(col_bits)],
         [floats(2, cols >> (k + 1), block_rows, lanes) for k in range(col_bits)],
-        sems(4),
+        sems(5 + 2 * slices),
         sems(8 * slices),
         sems(8 * slices),
         sems(8 * slices),
@@ -382,23 +441,23 @@
         sems(row_bits + col_bits),
         sems(row_bits + col_bits),
     ]
-    flops = slot_count * 6 * 2 * 3 * 2 * width * 4 * width * width
+    flops = slot_count * 6 * 2 * 3 * 2 * width * 2 * width * width
     return pl.pallas_call(
         kernel,
         out_shape=(
             jax.ShapeDtypeStruct(object_slices.shape, jnp.float32),
             jax.ShapeDtypeStruct((2, block_rows, block_cols), jnp.float32),
         ),
-        in_specs=[smem] * 2 + [vmem] * 4 + [pl.BlockSpec(memory_space=pl.ANY)],
+        in_specs=[smem] * 2 + [pl.BlockSpec(memory_space=pl.ANY)] * 6,
         out_specs=(vmem, vmem),
         scratch_shapes=scratch,
         compiler_params=pltpu.CompilerParams(
-            vmem_limit_bytes=52 * 2**20, collective_id=0, has_side_effects=True
+            vmem_limit_bytes=60 * 2**20, collective_id=0, has_side_effects=True
         ),
         cost_estimate=pl.CostEstimate(flops=flops, bytes_accessed=8 * 2**20, transcendentals=0),
     )(
         centres[0, 0], batch_order[0, 0], object_slices, probe_wave, propagator_phase,
-        intensity[0, 0], jnp.asarray(np.stack(tables(width))),
+        intensity[0, 0], jnp.asarray(constants), jnp.asarray(twiddles),
     )
 
 

time: 67.7 us -> 59.5 us (0.88)
  local copies, waits for them, and re-layouts: 6.4 us -> 2.29 us
  Pallas kernels: 60.3 us -> 56.4 us
    unnamed x14 -> x4, local copies, waits for them, and re-layouts: 6.4 us -> 2.29 us
    pallas_call x1, Pallas kernels: 60.3 us -> 56.4 us  [per_device(): pl.pallas_call(kernel, out_shape=(jax.ShapeDtypeStruct(object_slices.shap...]
where the time goes in v3:
time: 59.5 us; the launch traced here: 59.3 us
  Pallas kernels  56.4 us (95%)
  local copies, waits for them, and re-layouts  2.29 us (4%)
  between operations  0.65 us (1%)
    pallas_call x1, Pallas kernels, per_device(): pl.pallas_call(kernel, out_shape=(jax.ShapeDtypeStruct(object_slices.shap...  56.4 us
    unnamed x4, local copies, waits for them, and re-layouts  2.29 us

profile of v3, /device:TPU:0, one launch (start us, length us, event | category | flops | bytes accessed | tf_op | source)
XLA Modules:
  0.0 59.3 jit_solution(14915319352119463242)
XLA Ops:
  0.6 56.4 %shard_map.95 = (f32[2,2,128,128]{3,2,1,0:T(8,128)}, f32[2,32,64]{2,1,0:T(8,128)}) custom-call(s32[2,2]{1,0:T(2,128)} %bitcast.4, s32[2]{0:T(128)} %bitcast.5, f32[2,2,128,128]{3,2,1,0:T(8,128)} %tile.1, bf16[2,256,256]{2,1,0:T(8,128)(2,1)} %probe_hbm.1, bf16[256,256]{1,0:T(8,128)(2,1)} %phase_hbm.1, bf16[2,256,256]{2,1,0:T(8,128)(2,1)} %bitcast.3, ...), custom_call_target="tpu_custom_call" | custom-call | flops 4831838208 | bytes 8388608 | tf_op jit(solution)/shard_map/pallas_call | solution.py:445
  57.0 0.0 copy-start
  57.0 1.7 %copy.12 = f32[2,2,128,128]{3,2,1,0:T(8,128)} copy(f32[2,2,128,128]{3,2,1,0:T(8,128)} %get-tuple-element.4) | data formatting | bytes 524288
  58.7 0.0 copy-done
  58.7 0.6 %copy.13 = f32[2,32,64]{2,1,0:T(8,128)} copy(f32[2,32,64]{2,1,0:T(8,128)S(1)} %copy-done) | data formatting | bytes 32768
Async XLA Ops:
  57.0 1.7 %copy-start = (f32[2,32,64]{2,1,0:T(8,128)S(1)}, f32[2,32,64]{2,1,0:T(8,128)}, u32[]{:S(2)}) copy-start(f32[2,32,64]{2,1,0:T(8,128)} %get-tuple-element.5) | copy-start | bytes 49156

commit v4 on v3

--- a/solution.py
+++ b/solution.py
@@ -146,6 +146,30 @@
         if bit > 0:
             pl.semaphore_signal(barrier, inc=1, device_id={axis: partner(axis, bit)[1]}, device_id_type=MESH)
             count = count + 1
+
+    moves = [(tables_hbm, table), (phase_hbm, phase), (intensity_hbm, intensity), (turns_hbm, turns), (probe_hbm, probe)]
+    moves += [(tile.at[s, c], ext[s][c].at[middle, middle]) for s in range(slices) for c in range(2)]
+    loads = [pltpu.make_async_copy(src, dst, table_sem.at[k]) for k, (src, dst) in enumerate(moves)]
+    for load in loads:
+        load.start()
+
+    for s in range(slices):
+        for side, delta in enumerate((1, -1)):
+            place = first if delta > 0 else last
+
+            @pl.when(jnp.logical_not(has("row", -delta)))
+            def _(s=s, side=side, place=place):
+                ext[s][0][place, middle] = jnp.zeros((half, half), jnp.float32)
+                ext[s][1][place, every] = jnp.zeros((half, size), jnp.float32)
+                first_rows[s][side][...] = jnp.zeros((half, size), jnp.float32)
+                last_in[s][0][side][...] = jnp.zeros((half, half), jnp.float32)
+
+            @pl.when(jnp.logical_not(has("col", -delta)))
+            def _(s=s, side=side, place=place):
+                ext[s][1][middle, place] = jnp.zeros((half, half), jnp.float32)
+                ext[s][0][every, place] = jnp.zeros((size, half), jnp.float32)
+                first_cols[s][side][...] = jnp.zeros((size, half), jnp.float32)
+                last_in[s][1][side][...] = jnp.zeros((half, half), jnp.float32)
     pl.semaphore_wait(barrier, count)
 
     class Shift:
@@ -214,37 +238,10 @@
     folds = [[folding(s, part) for part in range(2)] for s in range(slices)]
     for s in range(slices):
         start_all(halos[s][0])
-    moves = [(tables_hbm, table), (phase_hbm, phase), (intensity_hbm, intensity), (turns_hbm, turns), (probe_hbm, probe)]
-    moves += [(tile.at[s, c], ext[s][c].at[middle, middle]) for s in range(slices) for c in range(2)]
-    loads = [pltpu.make_async_copy(src, dst, table_sem.at[k]) for k, (src, dst) in enumerate(moves)]
-    for load in loads:
-        load.start()
-
-    for s in range(slices):
-        for c in range(2):
-            acc[s][c][...] = jnp.zeros((size, size), jnp.float32)
-        for side, delta in enumerate((1, -1)):
-            place = first if delta > 0 else last
-
-            @pl.when(jnp.logical_not(has("row", -delta)))
-            def _(s=s, side=side, place=place):
-                ext[s][0][place, middle] = jnp.zeros((half, half), jnp.float32)
-                ext[s][1][place, every] = jnp.zeros((half, size), jnp.float32)
-                first_rows[s][side][...] = jnp.zeros((half, size), jnp.float32)
-                last_in[s][0][side][...] = jnp.zeros((half, half), jnp.float32)
-
-            @pl.when(jnp.logical_not(has("col", -delta)))
-            def _(s=s, side=side, place=place):
-                ext[s][1][middle, place] = jnp.zeros((half, half), jnp.float32)
-                ext[s][0][every, place] = jnp.zeros((size, half), jnp.float32)
-                first_cols[s][side][...] = jnp.zeros((size, half), jnp.float32)
-                last_in[s][1][side][...] = jnp.zeros((half, half), jnp.float32)
-
     for load in loads:
         load.wait()
-    for s in range(slices):
-        arrive_all(halos[s][0])
-        start_all(halos[s][1])
+    arrive_all(halos[0][0])
+    start_all(halos[0][1])
 
     def reordered(values):
         return dot(dot(table[4], values).astype(jnp.bfloat16), table[5])
@@ -255,6 +252,9 @@
     for slot in range(slot_count):
         measured[pl.ds(slot * width, width), :] = reordered(intensity[slot])
     arrive_all(halos[0][1])
+    for s in range(1, slices):
+        arrive_all(halos[s][0])
+        start_all(halos[s][1])
 
     transform = make_transform(table, turns, width, slot_count)
 
@@ -270,13 +270,19 @@
             parts.append(pltpu.roll(band, lax.rem(size - col, size), 1)[:, :width])
         return tuple(parts)
 
-    def place_term(s, slot, values):
-        row, col = start_of(slot)
+    def place_terms(s, values):
         for c in range(2):
-            wide = jnp.concatenate([values[c], jnp.zeros((width, size - width), jnp.float32)], axis=1)
-            wide = pltpu.roll(wide, col, 1)
-            tall = jnp.concatenate([wide, jnp.zeros((size - width, size), jnp.float32)], axis=0)
-            acc[s][c][...] += pltpu.roll(tall, row, 0)
+            total = None
+            for slot in range(slot_count):
+                row, col = start_of(slot)
+                value = values[c][slot * width : (slot + 1) * width]
+                wide = jnp.concatenate([value, jnp.zeros((width, size - width), jnp.float32)], axis=1)
+                wide = pltpu.roll(wide, col, 1)
+                tall = jnp.concatenate([wide, jnp.zeros((size - width, size), jnp.float32)], axis=0)
+                tall = pltpu.roll(tall, row, 0)
+                total = tall if total is None else total + tall
+            acc[s][c][...] = total
+            start_all(folds[s][0][c::2])
 
     def stack(pieces):
         return tuple(jnp.concatenate([piece[c] for piece in pieces], axis=0) for c in range(2))
@@ -293,11 +299,6 @@
 
     def propagator():
         return stack([pair(prop)] * slot_count)
-
-    def place_terms(s, values):
-        for slot in range(slot_count):
-            rows = slice(slot * width, (slot + 1) * width)
-            place_term(s, slot, (values[0][rows], values[1][rows]))
 
     keep(layer_zero, stack([window(0, slot) for slot in range(slot_count)]))
     spectrum = transform(product(entering_zero(), pair(layer_zero)), -1.0)
@@ -317,7 +318,6 @@
     adjoint = transform((misfit * spectrum[0], misfit * spectrum[1]), 1.0)
     place_terms(1, product(conjugate(pair(field_one)), adjoint))
     keep(upstream_one, product(conjugate(layer), adjoint))
-    start_all(folds[1][0])
 
     def fold_middle(s):
         arrive_all(folds[s][0])
@@ -377,7 +377,6 @@
     halvings[0][0].start()
 
     place_terms(0, product(conjugate(entering_zero()), adjoint))
-    start_all(folds[0][0])
     sum_next(0)
     fold_end(1)
     sum_next(1)

time: 59.5 us -> 60.7 us (1.020)
  Pallas kernels: 56.4 us -> 57.6 us
    pallas_call x1, Pallas kernels: 56.4 us -> 57.6 us  [per_device(): pl.pallas_call(kernel, out_shape=(jax.ShapeDtypeStruct(object_slices.shap...]
where the time goes in v4:
time: 60.7 us; the launch traced here: 60.5 us
  Pallas kernels  57.6 us (95%)
  local copies, waits for them, and re-layouts  2.29 us (4%)
  between operations  0.65 us (1%)
    pallas_call x1, Pallas kernels, per_device(): pl.pallas_call(kernel, out_shape=(jax.ShapeDtypeStruct(object_slices.shap...  57.6 us
    unnamed x4, local copies, waits for them, and re-layouts  2.29 us

profile of v4, /device:TPU:0, one launch (start us, length us, event | category | flops | bytes accessed | tf_op | source)
XLA Modules:
  0.0 60.5 jit_solution(6039039065176981068)
XLA Ops:
  0.6 57.6 %shard_map.95 = (f32[2,2,128,128]{3,2,1,0:T(8,128)}, f32[2,32,64]{2,1,0:T(8,128)}) custom-call(s32[2,2]{1,0:T(2,128)} %bitcast.4, s32[2]{0:T(128)} %bitcast.5, f32[2,2,128,128]{3,2,1,0:T(8,128)} %tile.1, bf16[2,256,256]{2,1,0:T(8,128)(2,1)} %probe_hbm.1, bf16[256,256]{1,0:T(8,128)(2,1)} %phase_hbm.1, bf16[2,256,256]{2,1,0:T(8,128)(2,1)} %bitcast.3, ...), custom_call_target="tpu_custom_call" | custom-call | flops 4831838208 | bytes 8388608 | tf_op jit(solution)/shard_map/pallas_call | solution.py:444
  58.2 0.0 copy-start
  58.2 1.7 %copy.12 = f32[2,2,128,128]{3,2,1,0:T(8,128)} copy(f32[2,2,128,128]{3,2,1,0:T(8,128)} %get-tuple-element.4) | data formatting | bytes 524288
  59.9 0.0 copy-done
  59.9 0.6 %copy.13 = f32[2,32,64]{2,1,0:T(8,128)} copy(f32[2,32,64]{2,1,0:T(8,128)S(1)} %copy-done) | data formatting | bytes 32768
Async XLA Ops:
  58.2 1.7 %copy-start = (f32[2,32,64]{2,1,0:T(8,128)S(1)}, f32[2,32,64]{2,1,0:T(8,128)}, u32[]{:S(2)}) copy-start(f32[2,32,64]{2,1,0:T(8,128)} %get-tuple-element.5) | copy-start | bytes 49156

commit v5 on v4

--- a/solution.py
+++ b/solution.py
@@ -240,8 +240,9 @@
         start_all(halos[s][0])
     for load in loads:
         load.wait()
-    arrive_all(halos[0][0])
-    start_all(halos[0][1])
+    for s in range(slices):
+        arrive_all(halos[s][0])
+        start_all(halos[s][1])
 
     def reordered(values):
         return dot(dot(table[4], values).astype(jnp.bfloat16), table[5])
@@ -252,9 +253,6 @@
     for slot in range(slot_count):
         measured[pl.ds(slot * width, width), :] = reordered(intensity[slot])
     arrive_all(halos[0][1])
-    for s in range(1, slices):
-        arrive_all(halos[s][0])
-        start_all(halos[s][1])
 
     transform = make_transform(table, turns, width, slot_count)
 

time: 60.7 us -> 59 us (0.972)
  Pallas kernels: 57.6 us -> 55.9 us
    pallas_call x1, Pallas kernels: 57.6 us -> 55.9 us  [per_device(): pl.pallas_call(kernel, out_shape=(jax.ShapeDtypeStruct(object_slices.shap...]
where the time goes in v5:
time: 59 us; the launch traced here: 58.8 us
  Pallas kernels  55.9 us (95%)
  local copies, waits for them, and re-layouts  2.29 us (4%)
  between operations  0.65 us (1%)
    pallas_call x1, Pallas kernels, per_device(): pl.pallas_call(kernel, out_shape=(jax.ShapeDtypeStruct(object_slices.shap...  55.9 us
    unnamed x4, local copies, waits for them, and re-layouts  2.29 us

profile of v5, /device:TPU:0, one launch (start us, length us, event | category | flops | bytes accessed | tf_op | source)
XLA Modules:
  0.0 58.8 jit_solution(14306014472145912114)
XLA Ops:
  0.6 55.9 %shard_map.95 = (f32[2,2,128,128]{3,2,1,0:T(8,128)}, f32[2,32,64]{2,1,0:T(8,128)}) custom-call(s32[2,2]{1,0:T(2,128)} %bitcast.4, s32[2]{0:T(128)} %bitcast.5, f32[2,2,128,128]{3,2,1,0:T(8,128)} %tile.1, bf16[2,256,256]{2,1,0:T(8,128)(2,1)} %probe_hbm.1, bf16[256,256]{1,0:T(8,128)(2,1)} %phase_hbm.1, bf16[2,256,256]{2,1,0:T(8,128)(2,1)} %bitcast.3, ...), custom_call_target="tpu_custom_call" | custom-call | flops 4831838208 | bytes 8388608 | tf_op jit(solution)/shard_map/pallas_call | solution.py:442
  56.5 0.0 copy-start
  56.5 1.7 %copy.12 = f32[2,2,128,128]{3,2,1,0:T(8,128)} copy(f32[2,2,128,128]{3,2,1,0:T(8,128)} %get-tuple-element.4) | data formatting | bytes 524288
  58.2 0.0 copy-done
  58.2 0.6 %copy.13 = f32[2,32,64]{2,1,0:T(8,128)} copy(f32[2,32,64]{2,1,0:T(8,128)S(1)} %copy-done) | data formatting | bytes 32768
Async XLA Ops:
  56.5 1.7 %copy-start = (f32[2,32,64]{2,1,0:T(8,128)S(1)}, f32[2,32,64]{2,1,0:T(8,128)}, u32[]{:S(2)}) copy-start(f32[2,32,64]{2,1,0:T(8,128)} %get-tuple-element.5) | copy-start | bytes 49156
